TPU v7x, 512 devices: a whole 4x4x16 slice. The times are simulated.
512 devices in a mesh: blk: 128 (over x_lo, y, z), rep: 4 (over x_hi, core).
Axes of the slice: x: 4 (x_hi: 2, x_lo: 2; x = x_hi * 2 + x_lo), y: 4, z: 16, core: 2. Of those that a mesh axis runs over, the one named last changes fastest.
Arguments:
- user_factors: float32 [2048, 128, 256], P('blk', 'rep'), may hold values from -6 to 6
- user_state: float32 [2048, 128], P('blk', 'rep'), may hold values from 0.1 to 4
- item_factors: float32 [3, 512, 128, 256], P(None, 'blk'), may hold values from -0.375 to 0.375
- item_state: float32 [3, 512, 128], P(None, 'blk'), may hold values from 0.05 to 2
- tile_lists: int32 [2, 16384, 4], P(None, 'blk'), may hold values from 0 to 15, as said below
- tile_counts: int32 [2, 128], P(None, 'blk'), may hold values from 1 to 128, as said below
- ratings: bfloat16 [2, 16384, 128, 128], P(None, 'blk', 'rep'), may hold values from -6 to 6
Outputs:
- users_out: float32 [2048, 128, 256], P('blk', 'rep')
- user_state_out: float32 [2048, 128], P('blk', 'rep')
- items_out: float32 [3, 512, 128, 256], P(None, 'blk')
- item_state_out: float32 [3, 512, 128], P(None, 'blk')
Inputs may be any that keep to these rules, and one draw needn't show every extreme that they name: `tile_lists`: column 0 is below 16, column 1 below 4, column 2 below 3, column 3 from 1 to 8. `tile_counts`: in each sub-epoch some stratum has all 128 slots live.
All inputs are finite; a program needn't handle non-finite values.
Results may differ from a plain program's by a relative error of at most 0.0032.
The roundings to bfloat16 on the way count: a program that leaves them out, or rounds other values in their place, can miss the bound.
Values sent between devices are 32-bit elements; how exact they have to be, the bound alone decides.
No kernel may reach another device: no remote copies, remote signals or barrier semaphores. Data moves between devices by JAX's collectives and lax.ppermute only.
A program may use at most 64 MiB of HBM per device.

v0:
```python
import jax
import jax.numpy as jnp
from jax import lax
from jax.sharding import PartitionSpec as P

decay_rate = 0.05
user_rate = 0.3
item_rate = 0.05


def from_behind(shard, axis, by):
    length = lax.axis_size(axis)
    return lax.ppermute(shard, axis, [(i, (i + by) % length) for i in range(length)])


def adagrad(param, state, grad, rate):
    full = grad + decay_rate * param
    state_new = state + jnp.mean(full * full, axis=-1)
    return (param - rate * full / jnp.sqrt(state_new)[..., None], state_new)


def tile_grads(users, items, lists, count, rates):
    width = users.shape[2]
    tiles_item = items.shape[1]
    columns = items.shape[2]
    slots = items.shape[0] * tiles_item
    users_low = users.astype(jnp.bfloat16)
    items_low = items.astype(jnp.bfloat16).reshape(slots, columns, width)
    block = 16
    turns = lists.shape[0] // block

    def step(carry, pack):
        grad_users, grad_items = carry
        entries, rate_block, first = pack
        live = first + jnp.arange(block, dtype=jnp.int32) < count
        weight = jnp.where(live, entries[:, 3].astype(jnp.float32) * 0.25, jnp.float32(0.0))
        slot = entries[:, 2] * tiles_item + entries[:, 1]
        user_index = entries[:, 0]
        user_tiles = jnp.take(users_low, user_index, axis=0)
        item_tiles = jnp.take(items_low, slot, axis=0)
        predicted = jnp.einsum(
            "nrk,nck->nrc", user_tiles, item_tiles, preferred_element_type=jnp.float32
        )
        error = (weight[:, None, None] * (predicted - rate_block.astype(jnp.float32))).astype(
            jnp.bfloat16
        )
        user_terms = jnp.einsum(
            "nrc,nck->nrk", error, item_tiles, preferred_element_type=jnp.float32
        )
        item_terms = jnp.einsum(
            "nrc,nrk->nck", error, user_tiles, preferred_element_type=jnp.float32
        )
        grad_users = grad_users.at[user_index].add(user_terms)
        grad_items = grad_items.at[slot].add(item_terms)
        return ((grad_users, grad_items), None)

    packs = (
        lists.reshape(turns, block, lists.shape[1]),
        rates.reshape(turns, block, rates.shape[1], rates.shape[2]),
        jnp.arange(turns, dtype=jnp.int32) * block,
    )
    start = (jnp.zeros(users.shape, jnp.float32), jnp.zeros((slots, columns, width), jnp.float32))
    (grad_users, grad_items), unused = lax.scan(step, start, packs)
    return (grad_users, grad_items.reshape(items.shape))


def per_device(
    user_factors, user_state, item_factors, item_state, tile_lists, tile_counts, ratings
):
    users, ustate = (user_factors, user_state)
    items, istate = (item_factors, item_state)
    for sweep in range(2):
        grad_users, grad_items = tile_grads(
            users, items, tile_lists[sweep], tile_counts[sweep, 0], ratings[sweep]
        )
        users, ustate = adagrad(users, ustate, grad_users, user_rate)
        summed = lax.psum(grad_items, "rep")
        items, istate = adagrad(items, istate, summed, item_rate)
        if sweep == 0:
            items, istate = from_behind((items, istate), "blk", 1)
    return (users, ustate, items, istate)


def solution(mesh):
    placed = (
        P("blk", "rep", None),
        P("blk", "rep"),
        P(None, "blk", None, None),
        P(None, "blk", None),
        P(None, "blk", None),
        P(None, "blk"),
        P(None, "blk", "rep", None),
    )
    return jax.shard_map(
        per_device,
        mesh=mesh,
        in_specs=placed,
        out_specs=(
            P("blk", "rep", None),
            P("blk", "rep"),
            P(None, "blk", None, None),
            P(None, "blk", None),
        ),
        check_vma=False,
    )
```

profile of v0, /device:TPU:1, one launch (start us, length us, event | category | flops | bytes accessed | tf_op | source)
XLA Modules:
  0.0 445.0 jit_solution(12901932321684276347)
XLA Ops:
  9.9 1.9 convert_element_type.46
  13.3 1.7 fusion.23
  16.4 115.6 %while.24 = (s32[]{:T(128)}, f32[16,32,256]{2,1,0:T(8,128)S(1)}, f32[12,128,256]{2,1,0:T(8,128)}, s32[8,16,4]{1,0,2:T(8,128)}, s32[8]{0:T(128)S(1)}, /*index=5*/...) while((s32[]{:T(128)}, f32[16,32,256]{2,1,0:T(8,128)S(1)}, ...), condition=%wide.region_3.6_spmd, body=%wide.region_0.5_spmd.sunk | while | flops 102894016 | bytes 17311748 | solution.py:63
  19.7 1.5 gather_fusion.1
  26.5 4.3 scatter_fusion.1
  34.1 1.5 gather_fusion.1
  40.9 4.3 scatter_fusion.1
  55.4 4.3 scatter_fusion.1
  63.0 1.5 gather_fusion.1
  69.8 4.2 scatter_fusion.1
  84.2 4.4 scatter_fusion.1
  98.8 4.4 scatter_fusion.1
  113.3 4.3 scatter_fusion.1
  127.7 4.3 scatter_fusion.1
  132.1 72.1 %all-reduce.3.cloned.1.call-done = f32[3,4,128,256]{3,2,1,0:T(8,128)} async-done(((f32[3,4,128,256]{3,2,1,0:T(8,128)}), f32[3,4,128,256]{3,2,1,0:T(8,128)}) %all-reduce.3.cloned.1.call-update) | async-done | bytes 1572880 | tf_op jit(solution)/shard_map/psum | solution.py:77
  204.2 1.8 multiply_reduce_fusion.1
  206.6 1.5 divide_subtract_fusion.1
  208.2 3.2 collective-permute-start
  212.7 38.1 %collective-permute-done = f32[3,4,128,256]{3,2,1,0:T(8,128)S(1)} collective-permute-done((f32[3,4,128,256]{3,2,1,0:T(8,128)}, f32[3,4,128,256]{3,2,1,0:T(8,128)S(1)}, u32[]{:S(2)}, u32[]{:S(2)}) %collective-permute-start) | collective-permute-done | bytes 1572896 | tf_op jit(solution)/shard_map/ppermute | solution.py:13
  252.5 118.5 %while.25 = (s32[]{:T(128)}, f32[16,32,256]{2,1,0:T(8,128)S(1)}, f32[12,128,256]{2,1,0:T(8,128)}, s32[8,16,4]{1,0,2:T(8,128)S(1)}, s32[8]{0:T(128)S(1)}, /*index...) while((s32[]{:T(128)}, f32[16,32,256]{2,1,0:T(8,128)S(1)}, ...), condition=%wide.region_10.13_spmd, body=%wide.region_7.12_spmd.sunk | while | flops 102894016 | bytes 17328500 | solution.py:63
  262.9 4.3 scatter_fusion.3
  277.7 4.3 scatter_fusion.3
  292.4 4.4 scatter_fusion.3
  307.3 4.4 scatter_fusion.3
  322.2 4.3 scatter_fusion.3
  336.9 4.3 scatter_fusion.3
  351.7 4.5 %scatter_fusion.3 = f32[12,128,256]{2,1,0:T(8,128)} fusion(f32[12,128,256]{2,1,0:T(8,128)} %get-tuple-element.362, s32[16]{0:T(128)S(1)} %get-tuple-element.319, f32[16,128,256]{2,1,0:T(8,128)S(1)} %fusion.53), kind=kCustom, calls=%fused_computation.7.clone.1 | custom fusion | flops 524288 | bytes 6291520 | tf_op jit(solution)/shard_map/while/body/eval_jaxpr/scatter-add | solution.py:54
  366.6 4.3 scatter_fusion.3
  371.6 1.9 collective-permute-start.1
  375.3 58.9 %all-reduce.5.cloned.1.call-done = f32[3,4,128,256]{3,2,1,0:T(8,128)} async-done(((f32[3,4,128,256]{3,2,1,0:T(8,128)}), f32[3,4,128,256]{3,2,1,0:T(8,128)}) %all-reduce.5.cloned.1.call-update) | async-done | bytes 1572880 | tf_op jit(solution)/shard_map/psum | solution.py:77
  434.2 1.8 multiply_reduce_fusion
  436.6 1.5 divide_subtract_fusion
  (365 shorter events, 170.6 us)
Async XLA Ops:
  7.2 197.0 %all-reduce.3.cloned.1.call-start = ((), (), s32[]{:S(2)}) async-start(), calls=%async_computation | async-start | bytes 3145728 | tf_op jit(solution)/shard_map/psum | solution.py:77
  132.0 72.2 %copy-start.2 = (f32[3,4,128,256]{3,2,1,0:T(8,128)S(1)}, f32[3,4,128,256]{3,2,1,0:T(8,128)}, u32[]{:S(2)}) copy-start(f32[3,4,128,256]{3,2,1,0:T(8,128)} %param.17) | copy-start | bytes 4718596
  132.1 74.0 %copy-start.14 = (f32[3,4,128]{2,1,0:T(4,128)S(1)}, f32[3,4,128]{2,1,0:T(4,128)}, u32[]{:S(2)}) copy-start(f32[3,4,128]{2,1,0:T(4,128)} %param.18) | copy-start | bytes 18436
  132.1 302.1 %all-reduce.5.cloned.1.call-start = ((), (), s32[]{:S(2)}) async-start(), calls=%async_computation.1 | async-start | bytes 3145728 | tf_op jit(solution)/shard_map/psum | solution.py:77
  206.6 4.8 %copy-start.8 = (f32[16,32,256]{2,1,0:T(8,128)S(1)}, f32[16,32,256]{2,1,0:T(8,128)}, u32[]{:S(2)}) copy-start(f32[16,32,256]{2,1,0:T(8,128)} %param.15) | copy-start | bytes 1572868
  206.6 5.0 %copy-start.12 = (f32[16,32]{1,0:T(8,128)S(1)}, f32[16,32]{1,0:T(8,128)}, u32[]{:S(2)}) copy-start(f32[16,32]{1,0:T(8,128)} %param.16) | copy-start | bytes 6148
  208.2 42.6 %collective-permute-start = (f32[3,4,128,256]{3,2,1,0:T(8,128)}, f32[3,4,128,256]{3,2,1,0:T(8,128)S(1)}, u32[]{:S(2)}, u32[]{:S(2)}) collective-permute-start(f32[3,4,128,256]{3,2,1,0:T(8,128)} %divide_subtract_fusion.1), channel_id=1, source_target_pairs={{0,4},{4,8},{8,12},{12,16},{16,20},{20,24},{24,28},{28,32},{32,36}... | collective-permute-start | bytes 4718600 | tf_op jit(solution)/shard_map/ppermute | solution.py:13
  252.5 5.1 %copy-start.10 = (s32[8,16,4]{1,0,2:T(8,128)}, s32[8,16,4]{1,0,2:T(8,128)S(1)}, u32[]{:S(2)}) copy-start(s32[8,16,4]{1,0,2:T(8,128)S(1)} %get-tuple-element.373) | copy-start | bytes 6148 | tf_op jit(solution)/shard_map/while
  262.9 4.4 copy-start.11
  262.9 4.3 copy-start.17
  267.3 5.1 %copy-start.10 = (s32[8,16,4]{1,0,2:T(8,128)}, s32[8,16,4]{1,0,2:T(8,128)S(1)}, u32[]{:S(2)}) copy-start(s32[8,16,4]{1,0,2:T(8,128)S(1)} %get-tuple-element.373) | copy-start | bytes 6148 | tf_op jit(solution)/shard_map/while
  277.7 4.3 copy-start.11
  282.0 5.1 %copy-start.10 = (s32[8,16,4]{1,0,2:T(8,128)}, s32[8,16,4]{1,0,2:T(8,128)S(1)}, u32[]{:S(2)}) copy-start(s32[8,16,4]{1,0,2:T(8,128)S(1)} %get-tuple-element.373) | copy-start | bytes 6148 | tf_op jit(solution)/shard_map/while
  292.4 4.5 %copy-start.11 = (s32[8,16,4]{1,0,2:T(8,128)S(1)}, s32[8,16,4]{1,0,2:T(8,128)}, u32[]{:S(2)}) copy-start(s32[8,16,4]{1,0,2:T(8,128)} %copy-done.10) | copy-start | bytes 6148 | tf_op jit(solution)/shard_map/while
  292.4 4.5 %copy-start.17 = (s32[8]{0:T(128)S(1)}, s32[8]{0:T(128)}, u32[]{:S(2)}) copy-start(s32[8]{0:T(128)} %copy-done.16) | copy-start | bytes 100 | tf_op jit(solution)/shard_map/while
  296.9 5.1 %copy-start.10 = (s32[8,16,4]{1,0,2:T(8,128)}, s32[8,16,4]{1,0,2:T(8,128)S(1)}, u32[]{:S(2)}) copy-start(s32[8,16,4]{1,0,2:T(8,128)S(1)} %get-tuple-element.373) | copy-start | bytes 6148 | tf_op jit(solution)/shard_map/while
  307.3 4.4 copy-start.11
  307.3 4.4 copy-start.17
  311.7 5.1 %copy-start.10 = (s32[8,16,4]{1,0,2:T(8,128)}, s32[8,16,4]{1,0,2:T(8,128)S(1)}, u32[]{:S(2)}) copy-start(s32[8,16,4]{1,0,2:T(8,128)S(1)} %get-tuple-element.373) | copy-start | bytes 6148 | tf_op jit(solution)/shard_map/while
  322.1 4.3 copy-start.11
  322.1 4.3 copy-start.17
  326.4 5.1 %copy-start.10 = (s32[8,16,4]{1,0,2:T(8,128)}, s32[8,16,4]{1,0,2:T(8,128)S(1)}, u32[]{:S(2)}) copy-start(s32[8,16,4]{1,0,2:T(8,128)S(1)} %get-tuple-element.373) | copy-start | bytes 6148 | tf_op jit(solution)/shard_map/while
  336.9 4.4 copy-start.11
  336.9 4.3 copy-start.17
  341.2 5.1 %copy-start.10 = (s32[8,16,4]{1,0,2:T(8,128)}, s32[8,16,4]{1,0,2:T(8,128)S(1)}, u32[]{:S(2)}) copy-start(s32[8,16,4]{1,0,2:T(8,128)S(1)} %get-tuple-element.373) | copy-start | bytes 6148 | tf_op jit(solution)/shard_map/while
  351.7 4.5 %copy-start.11 = (s32[8,16,4]{1,0,2:T(8,128)S(1)}, s32[8,16,4]{1,0,2:T(8,128)}, u32[]{:S(2)}) copy-start(s32[8,16,4]{1,0,2:T(8,128)} %copy-done.10) | copy-start | bytes 6148 | tf_op jit(solution)/shard_map/while
  351.7 4.5 %copy-start.17 = (s32[8]{0:T(128)S(1)}, s32[8]{0:T(128)}, u32[]{:S(2)}) copy-start(s32[8]{0:T(128)} %copy-done.16) | copy-start | bytes 100 | tf_op jit(solution)/shard_map/while
  356.2 5.1 %copy-start.10 = (s32[8,16,4]{1,0,2:T(8,128)}, s32[8,16,4]{1,0,2:T(8,128)S(1)}, u32[]{:S(2)}) copy-start(s32[8,16,4]{1,0,2:T(8,128)S(1)} %get-tuple-element.373) | copy-start | bytes 6148 | tf_op jit(solution)/shard_map/while
  366.6 4.3 copy-start.11
  366.6 4.3 copy-start.17
  371.0 63.2 %copy-start.4 = (f32[3,4,128,256]{3,2,1,0:T(8,128)S(1)}, f32[3,4,128,256]{3,2,1,0:T(8,128)}, u32[]{:S(2)}) copy-start(f32[3,4,128,256]{3,2,1,0:T(8,128)} %copy-done.3) | copy-start | bytes 4718596
  371.6 64.3 %collective-permute-start.1 = (f32[3,4,128]{2,1,0:T(4,128)S(1)}, f32[3,4,128]{2,1,0:T(4,128)S(1)}, u32[]{:S(2)}, u32[]{:S(2)}) collective-permute-start(f32[3,4,128]{2,1,0:T(4,128)S(1)} %copy-done.15), channel_id=1, source_target_pairs={{0,4},{4,8},{8,12},{12,16},{16,20},{20,24},{24,28},{28,32},{32,36}... | collective-permute-start | bytes 18440 | tf_op jit(solution)/shard_map/ppermute | solution.py:13
  (32 other events, 36.3 us)
Sparse Core Ops, SparseCore 0:
  132.2 71.9 all-reduce.2
  371.1 62.9 all-reduce.4
where the time goes:
time: 448 us; the launch traced here: 445 us
  waiting for transfers between devices  169 us (38%)
  other arithmetic  125 us (28%)
  local copies, waits for them, and re-layouts  78.6 us (18%)
  matrix products  51.6 us (12%)
  between operations  14.2 us (3%)
  starting transfers between devices  5.16 us (1%)
    psum x2, waiting for transfers between devices, per_device(): summed = lax.psum(grad_items, 'rep')  131 us
    scatter-add x16, other arithmetic, step(): grad_items = grad_items.at[slot].add(item_terms)  69.4 us
    ppermute x2, waiting for transfers between devices, from_behind(): lax.ppermute(shard, axis, [(i, (i + by) % length) for i in range(length)])  38.1 us
    gather x16, local copies, waits for them, and re-layouts, step(): user_tiles = jnp.take(users_low, user_index, axis=0)  24.2 us
    dot_general x16, matrix products, step(): jnp.einsum('nrc,nrk->nck', error, user_tiles, preferred_element_type=jnp....  23.3 us
    dot_general x16, matrix products, step(): jnp.einsum('nrk,nck->nrc', user_tiles, item_tiles, preferred_element_type...  22.9 us
    scatter-add x16, other arithmetic, step(): grad_users = grad_users.at[user_index].add(user_terms)  21.4 us
    dynamic_slice x32, local copies, waits for them, and re-layouts, tile_grads(): (grad_users, grad_items), unused = lax.scan(step, start, packs)  21 us
  transfers between devices with their start and end apart: 4, of which 3 were waited for; matrix products, arithmetic and copies ran while one was open for 1% of the time, Pallas kernels for 0%

commit v1 on v0

v1 whole, which is shorter than its diff:
```python
import functools

import jax
import jax.numpy as jnp
from jax import lax
from jax.experimental import pallas as pl
from jax.experimental.pallas import tpu as pltpu
from jax.sharding import PartitionSpec as P

decay_rate = 0.05
user_rate = 0.3
item_rate = 0.05

WIDTH = 256
TILE = 128
SLOTS = 12
HALF = SLOTS // 2
UTILES = 16
UROWS = 32
ROWS = UTILES * UROWS
CHUNKS = (6,)
OFFSETS = (0,)
UNROLL = 4
F32, BF16 = jnp.float32, jnp.bfloat16


def vmem(count):
    return [pl.BlockSpec(memory_space=pltpu.VMEM)] * count


def column_of(row):
    return jnp.broadcast_to(row, (TILE, TILE)).T[:, :1]


def row_of(column):
    return jnp.broadcast_to(column, (TILE, TILE)).T[:1, :]


def descend(param, state, grad, rate):
    full = grad + decay_rate * param
    state_new = state + jnp.mean(full * full, axis=-1, keepdims=True)
    return param - full * (rate / jnp.sqrt(state_new)), state_new


def places():
    rep = lax.axis_index("rep")
    return rep % 2, rep // 2


def grads_kernel(sweep, lists, count, ratings, users, *refs):
    n = len(CHUNKS)
    core, chip = places()
    if sweep == 0:
        items, refs = refs[0], refs[1:]
    else:
        same, cross, other, refs = refs[:n], refs[n : 2 * n], refs[2 * n : 3 * n], refs[3 * n :]
    send, keep, refs = refs[:n], refs[n : 2 * n], refs[2 * n :]
    errors, items_low, users_low, predicted, rates, users_in, *items_in, sems = refs

    copies = [
        pltpu.make_async_copy(users, users_in, sems.at[0]),
        pltpu.make_async_copy(ratings.at[sweep], rates, sems.at[1]),
    ]
    if sweep == 0:
        copies.append(pltpu.make_async_copy(items, items_in[0], sems.at[2]))
    for copy in (copies[0], *copies[2:], copies[1]):
        copy.start()
    errors[...] = jnp.zeros_like(errors)
    copies[0].wait()
    users_low[...] = users_in[...].reshape(ROWS, WIDTH).astype(BF16)
    if sweep == 0:
        copies[2].wait()
        items_low[...] = items_in[0][...].astype(BF16)
    else:
        for k in range(n):
            q = CHUNKS[k] // 2
            mine = core * HALF + OFFSETS[k]
            theirs = (1 - core) * HALF + OFFSETS[k]
            rows = q * TILE
            shape = (q, TILE, WIDTH)
            items_low[pl.ds(mine + chip * q, q)] = same[k][:rows].reshape(shape).astype(BF16)
            items_low[pl.ds(mine + (1 - chip) * q, q)] = (
                cross[k][:rows].reshape(shape).astype(BF16)
            )
            items_low[pl.ds(theirs + chip * q, q)] = other[k][:rows].reshape(shape).astype(BF16)
            items_low[pl.ds(theirs + (1 - chip) * q, q)] = (
                other[k][rows:].reshape(shape).astype(BF16)
            )

    for pair in range(SLOTS // 2):
        tiles = items_low[2 * pair : 2 * pair + 2].reshape(2 * TILE, WIDTH)
        product = lax.dot_general(
            users_low[...], tiles, (((1,), (1,)), ((), ())), preferred_element_type=F32
        )
        predicted[2 * pair] = product[:, :TILE]
        predicted[2 * pair + 1] = product[:, TILE:]
    copies[1].wait()

    live = count[0, sweep]

    def step(turn, carry):
        for lane in range(UNROLL):
            j = turn * UNROLL + lane
            row = pl.multiple_of(lists[sweep, 0, j] * UROWS, UROWS)
            slot = lists[sweep, 2, j] * 4 + lists[sweep, 1, j]
            weight = jnp.where(j < live, lists[sweep, 3, j].astype(F32) * 0.25, 0.0)
            guess = predicted[slot, pl.ds(row, UROWS), :]
            error = (weight * (guess - rates[j].astype(F32))).astype(BF16).astype(F32)
            errors[slot, pl.ds(row, UROWS), :] += error
        return carry

    lax.fori_loop(0, (live + UNROLL - 1) // UNROLL, step, 0)

    def gradient(tile):
        both = jnp.concatenate([errors[tile], errors[tile + 1]], axis=1)
        high = both.astype(BF16)
        low = (both - high.astype(F32)).astype(BF16)
        dims = (((0,), (0,)), ((), ()))
        return lax.dot_general(
            high, users_low[...], dims, preferred_element_type=F32
        ) + lax.dot_general(low, users_low[...], dims, preferred_element_type=F32)

    for k in range(n):
        for out, half in ((send[k], 1 - core), (keep[k], core)):
            for pair in range(CHUNKS[k] // 2):
                out[2 * TILE * pair : 2 * TILE * (pair + 1)] = gradient(
                    half * HALF + OFFSETS[k] + 2 * pair
                )


def users_kernel(errors, items_low, users, state, users_out, state_out):
    grad = jnp.zeros((ROWS, WIDTH), F32)
    for pair in range(SLOTS // 2):
        both = jnp.concatenate([errors[2 * pair], errors[2 * pair + 1]], axis=1)
        tiles = items_low[2 * pair : 2 * pair + 2].reshape(2 * TILE, WIDTH)
        high = both.astype(BF16)
        low = (both - high.astype(F32)).astype(BF16)
        grad += jnp.dot(high, tiles, preferred_element_type=F32)
        grad += jnp.dot(low, tiles, preferred_element_type=F32)
    lanes = lax.broadcasted_iota(jnp.int32, (UROWS, UTILES), 1)
    states = state[...].T
    out = jnp.zeros((UROWS, UTILES), F32)
    for tile in range(UTILES):
        new, column = descend(
            users[tile],
            states[:, tile : tile + 1],
            grad[tile * UROWS : (tile + 1) * UROWS],
            user_rate,
        )
        users_out[tile] = new
        out = jnp.where(lanes == tile, column, out)
    state_out[...] = out.T


def halves_kernel(after, keep, arrived, out, mine):
    del after
    core, chip = places()
    rows = out.shape[0]
    theirs = pl.ds(pl.multiple_of((1 - chip) * rows, TILE), rows)
    ours = pl.ds(pl.multiple_of(chip * rows, TILE), rows)
    out[...] = keep[theirs, :] + arrived[theirs, :]
    mine[...] = keep[ours, :] + arrived[ours, :]


def whole_kernel(after, keep, arrived, out):
    del after
    out[...] = keep[...] + arrived[...]


def first_step_kernel(tiles, mine, back, held, states, out):
    rows = tiles * TILE
    for tile in range(tiles):
        at = pl.ds(tile * TILE, TILE)
        new, column = descend(
            held[tile], column_of(states[tile : tile + 1, :]), mine[at, :] + back[at, :], item_rate
        )
        out[at, :] = new
        row = row_of(column)
        out[rows + tile : rows + tile + 1, :] = jnp.concatenate([row, row], axis=1)
    out[rows + tiles : rows + 8, :] = jnp.zeros((8 - tiles, WIDTH), F32)


def second_step_kernel(tiles, total, back, same, cross, out):
    _, chip = places()
    q = tiles // 2
    for tile in range(tiles):
        block, at = tile // q, tile % q
        source = (same, cross)[block]
        place = (chip if block == 0 else 1 - chip) * q + at
        rows = pl.ds(pl.multiple_of(place * TILE, TILE), TILE)
        new, column = descend(
            source[at * TILE : (at + 1) * TILE],
            column_of(source[q * TILE + at : q * TILE + at + 1, :TILE]),
            total[rows, :] + back[rows, :],
            item_rate,
        )
        out[tile * TILE : (tile + 1) * TILE, :] = new
        row = row_of(column)
        out[tiles * TILE + tile : tiles * TILE + tile + 1, :] = jnp.concatenate([row, row], axis=1)
    out[tiles * TILE + tiles : tiles * TILE + 8, :] = jnp.zeros((8 - tiles, WIDTH), F32)


def pack_kernel(after, same, cross, out):
    del after
    rows = out.shape[0] // 2
    out[:rows] = same[:rows]
    out[rows:] = cross[:rows]


def finish_kernel(*refs):
    n = len(CHUNKS)
    core, chip_at = places()
    own, other, (items_out, state_out) = refs[:n], refs[n : 2 * n], refs[2 * n :]
    for k in range(n):
        tiles = CHUNKS[k]
        q = tiles // 2
        for source, half in ((own[k], core), (other[k], 1 - core)):
            for tile in range(tiles):
                chip = chip_at if tile < q else 1 - chip_at
                place = half * HALF + OFFSETS[k] + chip * q + tile % q
                items_out[place] = source[tile * TILE : (tile + 1) * TILE]
                state_out[pl.ds(place, 1), :] = source[
                    tiles * TILE + tile : tiles * TILE + tile + 1, :TILE
                ]


def struct(*shape, dtype=F32):
    return jax.ShapeDtypeStruct(shape, dtype)


def call(body, name, in_specs, outs, *args, scratch=(), limit=8, work=2_000_000):
    return pl.pallas_call(
        body,
        out_shape=outs,
        in_specs=in_specs,
        out_specs=jax.tree.map(lambda _: pl.BlockSpec(memory_space=pltpu.VMEM), outs),
        scratch_shapes=scratch,
        compiler_params=pltpu.CompilerParams(vmem_limit_bytes=limit * 1024 * 1024),
        cost_estimate=pl.CostEstimate(flops=work, bytes_accessed=1_000_000, transcendentals=0),
        name=name,
    )(*args)


ANY = pl.BlockSpec(memory_space=pl.ANY)
SMEM = pl.BlockSpec(memory_space=pltpu.SMEM)


def run_grads(sweep, lists, count, ratings, users, parts):
    n = len(CHUNKS)
    shapes = [struct(t * TILE, WIDTH) for t in CHUNKS]
    scratch = [
        pltpu.VMEM((ROWS, WIDTH), BF16),
        pltpu.VMEM((SLOTS, ROWS, TILE), F32),
        pltpu.VMEM(ratings.shape[1:], BF16),
        pltpu.VMEM(users.shape, F32),
    ]
    if sweep == 0:
        scratch.append(pltpu.VMEM((SLOTS, TILE, WIDTH), F32))
    outs = call(
        functools.partial(grads_kernel, sweep),
        "grads",
        [SMEM, SMEM, ANY, ANY] + ([ANY] if sweep == 0 else vmem(len(parts))),
        shapes + shapes + [struct(SLOTS, ROWS, TILE), struct(SLOTS, TILE, WIDTH, dtype=BF16)],
        lists,
        count,
        ratings,
        users,
        *parts,
        scratch=scratch + [pltpu.SemaphoreType.DMA((3,))],
        limit=24,
        work=2_000_000_000,
    )
    return outs[:n], outs[n : 2 * n], outs[2 * n], outs[2 * n + 1]


def run_users(errors, items_low, users, state):
    return call(
        users_kernel,
        "users",
        vmem(4),
        [struct(*users.shape), struct(*state.shape)],
        errors,
        items_low,
        users,
        state,
        limit=16,
        work=1_000_000_000,
    )


def per_device(
    user_factors, user_state, item_factors, item_state, tile_lists, tile_counts, ratings
):
    n = len(CHUNKS)
    strata = lax.axis_size("blk")
    both = ("blk", "rep")
    core, chip = places()
    pairs = [(b, r) for b in range(strata) for r in range(4)]
    to_core = [(4 * b + r, 4 * b + (r ^ 1)) for b, r in pairs]
    to_chip = [(4 * b + r, 4 * b + (r ^ 2)) for b, r in pairs]
    on_same = [(4 * b + r, 4 * ((b + 1) % strata) + r) for b, r in pairs]
    on_cross = [(4 * b + r, 4 * ((b + 1) % strata) + (r ^ 2)) for b, r in pairs]

    items = item_factors.reshape(SLOTS, TILE, WIDTH)
    istate = item_state.reshape(SLOTS, TILE)
    lists = tile_lists.transpose(0, 2, 1)
    count = tile_counts.T

    send, keep, errors, low = run_grads(0, lists, count, ratings, user_factors, [items])
    arrived = [lax.ppermute(send[k], both, to_core) for k in range(n)]
    users, ustate = run_users(errors, low, user_factors, user_state)
    loads, same, cross, other = [], [], [], []
    for k in range(n):
        q = CHUNKS[k] // 2
        rows = q * TILE
        out, mine = call(
            halves_kernel,
            "halves",
            [ANY] + vmem(2),
            [struct(rows, WIDTH)] * 2,
            ustate,
            keep[k],
            arrived[k],
        )
        back = lax.ppermute(out, both, to_chip)
        tile = core * HALF + OFFSETS[k] + chip * q
        held = lax.dynamic_slice_in_dim(items, tile, q, 0)
        state = lax.dynamic_slice_in_dim(istate, tile, q, 0)
        load = call(
            functools.partial(first_step_kernel, q),
            "first_step",
            vmem(4),
            struct(rows + 8, WIDTH),
            mine,
            back,
            held,
            state,
        )
        loads.append(load)
        same.append(lax.ppermute(load, both, on_same))
        cross.append(lax.ppermute(load, both, on_cross))
    for k in range(n):
        rows = CHUNKS[k] // 2 * TILE
        whole = call(
            pack_kernel,
            "pack",
            [ANY] + vmem(2),
            struct(2 * rows, WIDTH),
            loads[-1],
            same[k],
            cross[k],
        )
        other.append(lax.ppermute(whole, both, to_core))

    send, keep, errors, low = run_grads(
        1, lists, count, ratings, users, [*same, *cross, *other]
    )
    arrived = [lax.ppermute(send[k], both, to_core) for k in range(n)]
    users, ustate = run_users(errors, low, users, ustate)
    own, rest = [], []
    for k in range(n):
        rows = CHUNKS[k] * TILE
        total = call(
            whole_kernel, "whole", [ANY] + vmem(2), struct(rows, WIDTH), ustate, keep[k], arrived[k]
        )
        back = lax.ppermute(total, both, to_chip)
        own.append(
            call(
                functools.partial(second_step_kernel, CHUNKS[k]),
                "second_step",
                vmem(4),
                struct(rows + 8, WIDTH),
                total,
                back,
                same[k],
                cross[k],
            )
        )
        rest.append(lax.ppermute(own[k], both, to_core))
    items_out, state_out = call(
        finish_kernel,
        "finish",
        vmem(2 * n),
        [struct(SLOTS, TILE, WIDTH), struct(SLOTS, TILE)],
        *own,
        *rest,
    )
    return (
        users,
        ustate,
        items_out.reshape(item_factors.shape),
        state_out.reshape(item_state.shape),
    )


def solution(mesh):
    placed = (
        P("blk", "rep", None),
        P("blk", "rep"),
        P(None, "blk", None, None),
        P(None, "blk", None),
        P(None, "blk", None),
        P(None, "blk"),
        P(None, "blk", "rep", None),
    )
    return jax.shard_map(
        per_device,
        mesh=mesh,
        in_specs=placed,
        out_specs=(
            P("blk", "rep", None),
            P("blk", "rep"),
            P(None, "blk", None, None),
            P(None, "blk", None),
        ),
        check_vma=False,
    )
```

time: 448 us -> 107 us (0.24)
  other arithmetic: 125 us -> 0 us
  waiting for transfers between devices: 169 us -> 57 us
  local copies, waits for them, and re-layouts: 78.6 us -> 7.89 us
  matrix products: 51.6 us -> 0 us
  starting transfers between devices: 5.16 us -> 27.2 us
  between operations: 14.2 us -> 0.83 us
  Pallas kernels: 0 us -> 13.1 us
    psum x2 -> x0, waiting for transfers between devices: 131 us -> none  [per_device(): summed = lax.psum(grad_items, 'rep')]
    scatter-add x32 -> x0, other arithmetic: 90.8 us -> none  [the longest x16 69.4 us: step(): grad_items = grad_items.at[slot].add(item_terms)]
    dot_general x48 -> x0, matrix products: 51.6 us -> none  [the longest x16 23.3 us: step(): jnp.einsum('nrc,nrk->nck', error, user_tiles, preferred_element_type=jnp....]
    gather x32 -> x0, local copies, waits for them, and re-layouts: 34 us -> none  [the longest x16 24.2 us: step(): user_tiles = jnp.take(users_low, user_index, axis=0)]
    ppermute x2 -> x8, starting transfers between devices: 5.08 us -> 27.2 us  [the longest x2 11.1 us: per_device(): arrived = [lax.ppermute(send[k], both, to_core) for k in range(n)]]
    dynamic_slice x32 -> x2, local copies, waits for them, and re-layouts: 21 us -> 1.18 us  [the longest x1 1.17 us: per_device(): held = lax.dynamic_slice_in_dim(items, tile, q, 0)]
    select_n x48 -> x0, other arithmetic: 19.1 us -> none  [the longest x16 18.9 us: step(): jnp.where(live, entries[:, 3].astype(jnp.float32) * 0.25, jnp.float32(0.0))]
    ppermute x2 -> x8, waiting for transfers between devices: 38.1 us -> 57 us  [the longest x1 19.3 us: per_device(): back = lax.ppermute(total, both, to_chip)]
  transfers between devices with their start and end apart: 4 -> 8, of which waited for: 3 -> 7; matrix products, arithmetic and copies ran while one was open for 1% -> 1% of each run, Pallas kernels for 0% -> 4%
where the time goes in v1:
time: 107 us; the launch traced here: 106 us
  waiting for transfers between devices  57 us (53%)
  starting transfers between devices  27.2 us (25%)
  Pallas kernels  13.1 us (12%)
  local copies, waits for them, and re-layouts  7.89 us (7%)
    ppermute x1, waiting for transfers between devices, per_device(): back = lax.ppermute(total, both, to_chip)  19.3 us
    ppermute x1, waiting for transfers between devices, per_device(): cross.append(lax.ppermute(load, both, on_cross))  15.1 us
    pallas_call x10, Pallas kernels, call(): pl.pallas_call(body, out_shape=outs, in_specs=in_specs, out_specs=jax.tre...  13.1 us
    ppermute x2, starting transfers between devices, per_device(): arrived = [lax.ppermute(send[k], both, to_core) for k in range(n)]  11.1 us
    ppermute x1, waiting for transfers between devices, per_device(): back = lax.ppermute(out, both, to_chip)  10.5 us
    ppermute x1, waiting for transfers between devices, per_device(): same.append(lax.ppermute(load, both, on_same))  8.15 us
    unnamed x22, local copies, waits for them, and re-layouts  6.1 us
    ppermute x1, starting transfers between devices, per_device(): other.append(lax.ppermute(whole, both, to_core))  3.85 us
  transfers between devices with their start and end apart: 8, of which 7 were waited for; matrix products, arithmetic and copies ran while one was open for 1% of the time, Pallas kernels for 4%

profile of v1, /device:TPU:1, one launch (start us, length us, event | category | flops | bytes accessed | tf_op | source)
XLA Modules:
  0.0 106.0 jit_solution(4698684251887942529)
XLA Ops:
  0.6 1.0 copy-done
  1.7 1.4 %copy-done.1 = f32[3,4,128,256]{3,2,1,0:T(8,128)S(1)} copy-done((f32[3,4,128,256]{3,2,1,0:T(8,128)S(1)}, f32[3,4,128,256]{3,2,1,0:T(8,128)}, u32[]{:S(2)}) %copy-start.1) | copy-done | bytes 1572888
  3.1 1.6 %copy-done.4 = bf16[2,128,32,128]{3,2,1,0:T(8,128)(2,1)S(1)} copy-done((bf16[2,128,32,128]{3,2,1,0:T(8,128)(2,1)S(1)}, bf16[2,128,32,128]{3,2,1,0:T(8,128)(2,1)}, u32[]{:S(2)}) %copy-start.4) | copy-done | bytes 2097176
  4.7 0.7 copy-done.6
  5.4 0.7 copy-done.8
  6.0 2.8 %grads.2 = (f32[768,256]{1,0:T(8,128)S(1)}, f32[768,256]{1,0:T(8,128)S(1)}, f32[12,512,128]{2,1,0:T(8,128)S(1)}, bf16[12,128,256]{2,1,0:T(8,128)(2,1)S(1)}) custom-call(s32[2,4,128]{2,1,0:T(4,128)S(1)} %bitcast.6, s32[1,2]{1,0:T(1,128)S(1)} %bitcast.8, bf16[2,128,32,128]{3,2,1,0:T(8,128)(2,1)S(1)} %copy-done.4, f32[16,32,256]{2,1,0:T(8,128)S(1)} %copy-done, ...), custom_call_target="tpu_custom_call" | custom-call | flops 2000000000 | bytes 1000000 | tf_op jit(solution)/shard_map/grads/pallas_call | solution.py:232
  8.9 8.8 %collective-permute-start = (f32[768,256]{1,0:T(8,128)S(1)}, f32[768,256]{1,0:T(8,128)S(1)}, u32[]{:S(2)}, u32[]{:S(2)}) collective-permute-start(f32[768,256]{1,0:T(8,128)S(1)} %get-tuple-element.25), channel_id=1, source_target_pairs={{0,1},{1,0},{2,3},{3,2},{4,5},{5,4},{6,7},{7,6},{8,9},{9,8},{10,11... | collective-permute-start | bytes 2359304 | tf_op jit(solution)/shard_map/ppermute | solution.py:310
  17.7 1.8 %users.5 = (f32[16,32,256]{2,1,0:T(8,128)S(1)}, f32[16,32]{1,0:T(8,128)S(1)}) custom-call(f32[12,512,128]{2,1,0:T(8,128)S(1)} %get-tuple-element.20.errors, bf16[12,128,256]{2,1,0:T(8,128)(2,1)S(1)} %get-tuple-element.21.items_low, f32[16,32,256]{2,1,0:T(8,128)S(1)} %copy-done, f32[16,32]{1,0:T(8,128)S(1)} %copy-done.2), custom_call_target="tpu_custom_call" | custom-call | flops 1000000000 | bytes 1000000 | tf_op jit(solution)/shard_map/users/pallas_call | solution.py:232
  19.4 0.1 collective-permute-done.arrived
  19.5 0.1 halves.1
  19.7 1.9 %collective-permute-start.1 = (f32[384,256]{1,0:T(8,128)S(1)}, f32[384,256]{1,0:T(8,128)S(1)}, u32[]{:S(2)}, u32[]{:S(2)}) collective-permute-start(f32[384,256]{1,0:T(8,128)S(1)} %get-tuple-element.27), channel_id=1, source_target_pairs={{0,2},{1,3},{2,0},{3,1},{4,6},{5,7},{6,4},{7,5},{8,10},{9,11},{10,... | collective-permute-start | bytes 1179656 | tf_op jit(solution)/shard_map/ppermute | solution.py:325
  21.7 1.2 %constant_dynamic-slice_fusion.1.held = f32[3,128,256]{2,1,0:T(8,128)S(1)} fusion(f32[12,128,256]{2,1,0:T(8,128)} %bitcast.4, s32[]{:T(128)S(6)} %select_n.17), kind=kLoop, calls=%fused_computation.1 | loop fusion | bytes 786436 | tf_op jit(solution)/shard_map/dynamic_slice | solution.py:327
  22.9 10.5 %collective-permute-done.1.back = f32[384,256]{1,0:T(8,128)S(1)} collective-permute-done((f32[384,256]{1,0:T(8,128)S(1)}, f32[384,256]{1,0:T(8,128)S(1)}, u32[]{:S(2)}, u32[]{:S(2)}) %collective-permute-start.1) | collective-permute-done | bytes 393248 | tf_op jit(solution)/shard_map/ppermute | solution.py:325
  33.4 0.5 first_step.1.after
  33.8 1.9 %collective-permute-start.3 = (f32[392,256]{1,0:T(8,128)S(1)}, f32[392,256]{1,0:T(8,128)S(1)}, u32[]{:S(2)}, u32[]{:S(2)}) collective-permute-start(f32[392,256]{1,0:T(8,128)S(1)} %first_step.1.after), channel_id=1, source_target_pairs={{0,6},{1,7},{2,4},{3,5},{4,10},{5,11},{6,8},{7,9},{8,14},{9,15},{1... | collective-permute-start | bytes 1204232 | tf_op jit(solution)/shard_map/ppermute | solution.py:341
  35.8 2.5 %collective-permute-start.2 = (f32[392,256]{1,0:T(8,128)S(1)}, f32[392,256]{1,0:T(8,128)S(1)}, u32[]{:S(2)}, u32[]{:S(2)}) collective-permute-start(f32[392,256]{1,0:T(8,128)S(1)} %first_step.1.after), channel_id=1, source_target_pairs={{0,4},{1,5},{2,6},{3,7},{4,8},{5,9},{6,10},{7,11},{8,12},{9,13},{1... | collective-permute-start | bytes 1204232 | tf_op jit(solution)/shard_map/ppermute | solution.py:340
  38.3 15.1 %collective-permute-done.3.cross.refs_1_ = f32[392,256]{1,0:T(8,128)S(1)} collective-permute-done((f32[392,256]{1,0:T(8,128)S(1)}, f32[392,256]{1,0:T(8,128)S(1)}, u32[]{:S(2)}, u32[]{:S(2)}) %collective-permute-start.3) | collective-permute-done | bytes 401440 | tf_op jit(solution)/shard_map/ppermute | solution.py:341
  53.3 8.2 %collective-permute-done.2.same.refs_0_ = f32[392,256]{1,0:T(8,128)S(1)} collective-permute-done((f32[392,256]{1,0:T(8,128)S(1)}, f32[392,256]{1,0:T(8,128)S(1)}, u32[]{:S(2)}, u32[]{:S(2)}) %collective-permute-start.2) | collective-permute-done | bytes 401440 | tf_op jit(solution)/shard_map/ppermute | solution.py:340
  61.6 3.8 %collective-permute-start.4 = (f32[768,256]{1,0:T(8,128)S(1)}, f32[768,256]{1,0:T(8,128)S(1)}, u32[]{:S(2)}, u32[]{:S(2)}) collective-permute-start(f32[768,256]{1,0:T(8,128)S(1)} %pack.1), channel_id=1, source_target_pairs={{0,1},{1,0},{2,3},{3,2},{4,5},{5,4},{6,7},{7,6},{8,9},{9,8},{10,11... | collective-permute-start | bytes 2359304 | tf_op jit(solution)/shard_map/ppermute | solution.py:353
  65.4 1.9 %collective-permute-done.4.refs_2_ = f32[768,256]{1,0:T(8,128)S(1)} collective-permute-done((f32[768,256]{1,0:T(8,128)S(1)}, f32[768,256]{1,0:T(8,128)S(1)}, u32[]{:S(2)}, u32[]{:S(2)}) %collective-permute-start.4) | collective-permute-done | bytes 786464 | tf_op jit(solution)/shard_map/ppermute | solution.py:353
  67.3 3.3 %grads.3 = (f32[768,256]{1,0:T(8,128)S(1)}, f32[768,256]{1,0:T(8,128)S(1)}, f32[12,512,128]{2,1,0:T(8,128)S(1)}, bf16[12,128,256]{2,1,0:T(8,128)(2,1)S(1)}) custom-call(s32[2,4,128]{2,1,0:T(4,128)S(1)} %bitcast.7, s32[1,2]{1,0:T(1,128)S(1)} %bitcast.9, bf16[2,128,32,128]{3,2,1,0:T(8,128)(2,1)S(1)} %copy-done.5, f32[16,32,256]{2,1,0:T(8,128)S(1)} %get-tuple-element.22.users, ...), custom_call_target="tpu_custom_call" | custom-call | flops 2000000000 | bytes 1000000 | tf_op jit(solution)/shard_map/grads/pallas_call | solution.py:232
  70.6 2.3 %collective-permute-start.5 = (f32[768,256]{1,0:T(8,128)S(1)}, f32[768,256]{1,0:T(8,128)S(1)}, u32[]{:S(2)}, u32[]{:S(2)}) collective-permute-start(f32[768,256]{1,0:T(8,128)S(1)} %get-tuple-element.33), channel_id=1, source_target_pairs={{0,1},{1,0},{2,3},{3,2},{4,5},{5,4},{6,7},{7,6},{8,9},{9,8},{10,11... | collective-permute-start | bytes 2359304 | tf_op jit(solution)/shard_map/ppermute | solution.py:358
  72.9 2.5 %users.7 = (f32[16,32,256]{2,1,0:T(8,128)}, f32[16,32]{1,0:T(8,128)}) custom-call(f32[12,512,128]{2,1,0:T(8,128)S(1)} %get-tuple-element.28.errors, bf16[12,128,256]{2,1,0:T(8,128)(2,1)S(1)} %get-tuple-element.29.items_low, f32[16,32,256]{2,1,0:T(8,128)S(1)} %get-tuple-element.22.users, f32[16,32]{1,0:T(8,128)S(1)} %get-tuple-element.23.after.state), custom_call_target="tpu_custom_call" | custom-call | flops 1000000000 | bytes 1000000 | tf_op jit(solution)/shard_map/users/pallas_call | solution.py:232
  75.4 0.7 copy-done.3
  76.1 0.1 whole.1.total
  76.2 3.1 %collective-permute-start.6 = (f32[768,256]{1,0:T(8,128)S(1)}, f32[768,256]{1,0:T(8,128)S(1)}, u32[]{:S(2)}, u32[]{:S(2)}) collective-permute-start(f32[768,256]{1,0:T(8,128)S(1)} %whole.1.total), channel_id=1, source_target_pairs={{0,2},{1,3},{2,0},{3,1},{4,6},{5,7},{6,4},{7,5},{8,10},{9,11},{10,... | collective-permute-start | bytes 2359304 | tf_op jit(solution)/shard_map/ppermute | solution.py:366
  79.3 19.3 %collective-permute-done.6.back = f32[768,256]{1,0:T(8,128)S(1)} collective-permute-done((f32[768,256]{1,0:T(8,128)S(1)}, f32[768,256]{1,0:T(8,128)S(1)}, u32[]{:S(2)}, u32[]{:S(2)}) %collective-permute-start.6) | collective-permute-done | bytes 786464 | tf_op jit(solution)/shard_map/ppermute | solution.py:366
  98.6 0.8 second_step.1.refs_0_
  99.4 2.9 %collective-permute-start.7 = (f32[776,256]{1,0:T(8,128)S(1)}, f32[776,256]{1,0:T(8,128)S(1)}, u32[]{:S(2)}, u32[]{:S(2)}) collective-permute-start(f32[776,256]{1,0:T(8,128)S(1)} %second_step.1.refs_0_), channel_id=1, source_target_pairs={{0,1},{1,0},{2,3},{3,2},{4,5},{5,4},{6,7},{7,6},{8,9},{9,8},{10,11... | collective-permute-start | bytes 2383880 | tf_op jit(solution)/shard_map/ppermute | solution.py:379
  102.3 1.9 %collective-permute-done.7.refs_1_ = f32[776,256]{1,0:T(8,128)S(1)} collective-permute-done((f32[776,256]{1,0:T(8,128)S(1)}, f32[776,256]{1,0:T(8,128)S(1)}, u32[]{:S(2)}, u32[]{:S(2)}) %collective-permute-start.7) | collective-permute-done | bytes 794656 | tf_op jit(solution)/shard_map/ppermute | solution.py:379
  104.2 1.3 %finish.1 = (f32[12,128,256]{2,1,0:T(8,128)}, f32[12,128]{1,0:T(8,128)S(1)}) custom-call(f32[776,256]{1,0:T(8,128)S(1)} %second_step.1.refs_0_, f32[776,256]{1,0:T(8,128)S(1)} %collective-permute-done.7.refs_1_), custom_call_target="tpu_custom_call" | custom-call | flops 2000000 | bytes 1000000 | tf_op jit(solution)/shard_map/finish/pallas_call | solution.py:232
  105.4 0.6 reshape.23
  (20 shorter events, 0.1 us)
Async XLA Ops:
  0.6 1.0 copy-start
  1.7 1.4 %copy-start.1 = (f32[3,4,128,256]{3,2,1,0:T(8,128)S(1)}, f32[3,4,128,256]{3,2,1,0:T(8,128)}, u32[]{:S(2)}) copy-start(f32[3,4,128,256]{3,2,1,0:T(8,128)} %param.9) | copy-start | bytes 4718596
  3.1 1.6 %copy-start.4 = (bf16[2,128,32,128]{3,2,1,0:T(8,128)(2,1)S(1)}, bf16[2,128,32,128]{3,2,1,0:T(8,128)(2,1)}, u32[]{:S(2)}) copy-start(bf16[2,128,32,128]{3,2,1,0:T(8,128)(2,1)} %ratings.3) | copy-start | bytes 6291460
  4.7 0.7 copy-start.6
  5.4 0.7 copy-start.8
  6.0 11.6 %copy-start.2 = (f32[16,32]{1,0:T(8,128)S(1)}, f32[16,32]{1,0:T(8,128)}, u32[]{:S(2)}) copy-start(f32[16,32]{1,0:T(8,128)} %state.1) | copy-start | bytes 6148
  8.9 10.7 %collective-permute-start = (f32[768,256]{1,0:T(8,128)S(1)}, f32[768,256]{1,0:T(8,128)S(1)}, u32[]{:S(2)}, u32[]{:S(2)}) collective-permute-start(f32[768,256]{1,0:T(8,128)S(1)} %get-tuple-element.25), channel_id=1, source_target_pairs={{0,1},{1,0},{2,3},{3,2},{4,5},{5,4},{6,7},{7,6},{8,9},{9,8},{10,11... | collective-permute-start | bytes 2359304 | tf_op jit(solution)/shard_map/ppermute | solution.py:310
  17.7 3.9 %copy-start.10 = (f32[3,4,128]{2,1,0:T(4,128)S(1)}, f32[3,4,128]{2,1,0:T(4,128)}, u32[]{:S(2)}) copy-start(f32[3,4,128]{2,1,0:T(4,128)} %param.10) | copy-start | bytes 18436
  19.7 13.7 %collective-permute-start.1 = (f32[384,256]{1,0:T(8,128)S(1)}, f32[384,256]{1,0:T(8,128)S(1)}, u32[]{:S(2)}, u32[]{:S(2)}) collective-permute-start(f32[384,256]{1,0:T(8,128)S(1)} %get-tuple-element.27), channel_id=1, source_target_pairs={{0,2},{1,3},{2,0},{3,1},{4,6},{5,7},{6,4},{7,5},{8,10},{9,11},{10,... | collective-permute-start | bytes 1179656 | tf_op jit(solution)/shard_map/ppermute | solution.py:325
  21.7 45.6 %copy-start.5 = (bf16[2,128,32,128]{3,2,1,0:T(8,128)(2,1)S(1)}, bf16[2,128,32,128]{3,2,1,0:T(8,128)(2,1)}, u32[]{:S(2)}) copy-start(bf16[2,128,32,128]{3,2,1,0:T(8,128)(2,1)} %ratings.3) | copy-start | bytes 6291460
  21.7 45.6 %copy-start.7 = (s32[2,128,4]{1,2,0:T(4,128)S(1)}, s32[2,128,4]{1,2,0:T(4,128)}, u32[]{:S(2)}) copy-start(s32[2,128,4]{1,2,0:T(4,128)} %param.11) | copy-start | bytes 12292
  21.7 45.6 %copy-start.9 = (s32[2,1]{0,1:T(1,128)S(1)}, s32[2,1]{0,1:T(1,128)}, u32[]{:S(2)}) copy-start(s32[2,1]{0,1:T(1,128)} %param.12) | copy-start | bytes 28
  33.8 19.5 %collective-permute-start.3 = (f32[392,256]{1,0:T(8,128)S(1)}, f32[392,256]{1,0:T(8,128)S(1)}, u32[]{:S(2)}, u32[]{:S(2)}) collective-permute-start(f32[392,256]{1,0:T(8,128)S(1)} %first_step.1.after), channel_id=1, source_target_pairs={{0,6},{1,7},{2,4},{3,5},{4,10},{5,11},{6,8},{7,9},{8,14},{9,15},{1... | collective-permute-start | bytes 1204232 | tf_op jit(solution)/shard_map/ppermute | solution.py:341
  35.8 25.7 %collective-permute-start.2 = (f32[392,256]{1,0:T(8,128)S(1)}, f32[392,256]{1,0:T(8,128)S(1)}, u32[]{:S(2)}, u32[]{:S(2)}) collective-permute-start(f32[392,256]{1,0:T(8,128)S(1)} %first_step.1.after), channel_id=1, source_target_pairs={{0,4},{1,5},{2,6},{3,7},{4,8},{5,9},{6,10},{7,11},{8,12},{9,13},{1... | collective-permute-start | bytes 1204232 | tf_op jit(solution)/shard_map/ppermute | solution.py:340
  61.6 5.7 %collective-permute-start.4 = (f32[768,256]{1,0:T(8,128)S(1)}, f32[768,256]{1,0:T(8,128)S(1)}, u32[]{:S(2)}, u32[]{:S(2)}) collective-permute-start(f32[768,256]{1,0:T(8,128)S(1)} %pack.1), channel_id=1, source_target_pairs={{0,1},{1,0},{2,3},{3,2},{4,5},{5,4},{6,7},{7,6},{8,9},{9,8},{10,11... | collective-permute-start | bytes 2359304 | tf_op jit(solution)/shard_map/ppermute | solution.py:353
  70.6 4.8 %collective-permute-start.5 = (f32[768,256]{1,0:T(8,128)S(1)}, f32[768,256]{1,0:T(8,128)S(1)}, u32[]{:S(2)}, u32[]{:S(2)}) collective-permute-start(f32[768,256]{1,0:T(8,128)S(1)} %get-tuple-element.33), channel_id=1, source_target_pairs={{0,1},{1,0},{2,3},{3,2},{4,5},{5,4},{6,7},{7,6},{8,9},{9,8},{10,11... | collective-permute-start | bytes 2359304 | tf_op jit(solution)/shard_map/ppermute | solution.py:358
  75.4 0.7 copy-start.3
  76.2 22.4 %collective-permute-start.6 = (f32[768,256]{1,0:T(8,128)S(1)}, f32[768,256]{1,0:T(8,128)S(1)}, u32[]{:S(2)}, u32[]{:S(2)}) collective-permute-start(f32[768,256]{1,0:T(8,128)S(1)} %whole.1.total), channel_id=1, source_target_pairs={{0,2},{1,3},{2,0},{3,1},{4,6},{5,7},{6,4},{7,5},{8,10},{9,11},{10,... | collective-permute-start | bytes 2359304 | tf_op jit(solution)/shard_map/ppermute | solution.py:366
  99.4 4.8 %collective-permute-start.7 = (f32[776,256]{1,0:T(8,128)S(1)}, f32[776,256]{1,0:T(8,128)S(1)}, u32[]{:S(2)}, u32[]{:S(2)}) collective-permute-start(f32[776,256]{1,0:T(8,128)S(1)} %second_step.1.refs_0_), channel_id=1, source_target_pairs={{0,1},{1,0},{2,3},{3,2},{4,5},{5,4},{6,7},{7,6},{8,9},{9,8},{10,11... | collective-permute-start | bytes 2383880 | tf_op jit(solution)/shard_map/ppermute | solution.py:379

commit v2 on v0

v2 whole, which is shorter than its diff:
```python
import functools

import jax
import jax.numpy as jnp
from jax import lax
from jax.experimental import pallas as pl
from jax.experimental.pallas import tpu as pltpu
from jax.sharding import PartitionSpec as P

decay_rate = 0.05
user_rate = 0.3
item_rate = 0.05

WIDTH = 256
TILE = 128
SLOTS = 12
HALF = SLOTS // 2
UTILES = 16
UROWS = 32
ROWS = UTILES * UROWS
SPLIT = 4
SHARE = HALF * TILE
UNROLL = 4
PARTS = ((0, 4), (4, 2))
RELAY_WORK = 10_000_000_000
LIMITS = (54, 24)
F32, BF16 = jnp.float32, jnp.bfloat16


def column_of(row):
    return jnp.broadcast_to(row, (TILE, TILE)).T[:, :1]


def row_of(column):
    return jnp.broadcast_to(column, (TILE, TILE)).T[:1, :]


def descend(param, state, grad, rate):
    full = grad + decay_rate * param
    state_new = state + jnp.mean(full * full, axis=-1, keepdims=True)
    return param - full * (rate / jnp.sqrt(state_new)), state_new


def places():
    rep = lax.axis_index("rep")
    return rep % 2, rep // 2


def put_state(out, row, column):
    line = row_of(column)
    out[row : row + 1, :] = jnp.concatenate([line, line], axis=1)


def grads_kernel(sweep, lists, count, ratings, users, *refs):
    core, _ = places()
    if sweep == 0:
        items, send, keep, *refs = refs
    else:
        own, other, send, keep, *refs = refs
    errors, items_low, list_in, count_in, users_low, predicted, rates, users_in, sems, *rest = refs
    leaving = []
    if sweep == 0:
        items_in, *staged, out_sems = rest
        outs = (send, keep, errors, items_low)
        send, keep, errors, items_low = staged

    def leave(which, rows=None):
        if sweep == 0:
            source, target = staged[which], outs[which]
            if rows is not None:
                source, target = source.at[rows, :], target.at[rows, :]
            copy = pltpu.make_async_copy(source, target, out_sems.at[len(leaving)])
            copy.start()
            leaving.append(copy)

    copies = [
        pltpu.make_async_copy(users, users_in, sems.at[0]),
        pltpu.make_async_copy(ratings.at[sweep], rates, sems.at[1]),
        pltpu.make_async_copy(lists.at[sweep], list_in, sems.at[2]),
        pltpu.make_async_copy(count, count_in, sems.at[3]),
    ]
    if sweep == 0:
        copies.append(pltpu.make_async_copy(items, items_in, sems.at[4]))
    for copy in (copies[0], *copies[4:], *copies[1:4]):
        copy.start()
    errors[...] = jnp.zeros_like(errors)
    copies[0].wait()
    users_low[...] = users_in[...].reshape(ROWS, WIDTH).astype(BF16)
    if sweep == 0:
        copies[4].wait()
        items_low[...] = items_in[...].astype(BF16)
    else:
        shape = (HALF, TILE, WIDTH)
        items_low[pl.ds(core * HALF, HALF)] = own[:SHARE].reshape(shape).astype(BF16)
        items_low[pl.ds((1 - core) * HALF, HALF)] = other[:SHARE].reshape(shape).astype(BF16)

    leave(3)
    for pair in range(SLOTS // 2):
        tiles = items_low[2 * pair : 2 * pair + 2].reshape(2 * TILE, WIDTH)
        product = lax.dot_general(
            users_low[...], tiles, (((1,), (1,)), ((), ())), preferred_element_type=F32
        )
        predicted[2 * pair] = product[:, :TILE]
        predicted[2 * pair + 1] = product[:, TILE:]
    for copy in copies[1:4]:
        copy.wait()

    live = count_in[0, sweep]

    def step(turn, carry):
        for lane in range(UNROLL):
            j = turn * UNROLL + lane
            row = pl.multiple_of(list_in[0, j] * UROWS, UROWS)
            slot = list_in[2, j] * 4 + list_in[1, j]
            weight = jnp.where(j < live, list_in[3, j].astype(F32) * 0.25, 0.0)
            guess = predicted[slot, pl.ds(row, UROWS), :]
            error = (weight * (guess - rates[j].astype(F32))).astype(BF16).astype(F32)
            errors[slot, pl.ds(row, UROWS), :] += error
        return carry

    lax.fori_loop(0, (live + UNROLL - 1) // UNROLL, step, 0)
    leave(2)

    def gradient(tile):
        both = jnp.concatenate([errors[tile], errors[tile + 1]], axis=1)
        high = both.astype(BF16)
        low = (both - high.astype(F32)).astype(BF16)
        dims = (((0,), (0,)), ((), ()))
        return lax.dot_general(
            high, users_low[...], dims, preferred_element_type=F32
        ) + lax.dot_general(low, users_low[...], dims, preferred_element_type=F32)

    for which, (out, half) in enumerate(((send, 1 - core), (keep, core))):
        for pair in range(HALF // 2):
            rows = pl.ds(2 * TILE * pair, 2 * TILE)
            out[rows, :] = gradient(half * HALF + 2 * pair)
            leave(which, rows)
    for copy in leaving:
        copy.wait()


def olds_kernel(keep, items, states, kept, hold, early):
    core, _ = places()
    kept[...] = keep[...]
    for out, first, tiles in ((hold, 0, SPLIT), (early, SPLIT, HALF - SPLIT)):
        rows = tiles * TILE
        base = core * HALF + first
        out[:rows] = items[pl.ds(base, tiles)].reshape(rows, WIDTH)
        for tile in range(tiles):
            place = base + tile
            line = states[place // 4, pl.ds(place % 4, 1), :]
            out[rows + tile : rows + tile + 1, :] = jnp.concatenate([line, line], axis=1)
        out[rows + tiles : rows + 8, :] = jnp.zeros((8 - tiles, WIDTH), F32)


def users_kernel(after, errors, items_low, users, state, users_out, state_out, token):
    del after
    token[...] = jnp.zeros_like(token)
    grad = jnp.zeros((ROWS, WIDTH), F32)
    for pair in range(SLOTS // 2):
        both = jnp.concatenate([errors[2 * pair], errors[2 * pair + 1]], axis=1)
        tiles = items_low[2 * pair : 2 * pair + 2].reshape(2 * TILE, WIDTH)
        high = both.astype(BF16)
        low = (both - high.astype(F32)).astype(BF16)
        grad += jnp.dot(high, tiles, preferred_element_type=F32)
        grad += jnp.dot(low, tiles, preferred_element_type=F32)
    lanes = lax.broadcasted_iota(jnp.int32, (UROWS, UTILES), 1)
    states = state[...].T
    out = jnp.zeros((UROWS, UTILES), F32)
    for tile in range(UTILES):
        new, column = descend(
            users[tile],
            states[:, tile : tile + 1],
            grad[tile * UROWS : (tile + 1) * UROWS],
            user_rate,
        )
        users_out[tile] = new
        out = jnp.where(lanes == tile, column, out)
    state_out[...] = out.T


def parts_kernel(keep, arrived, near, far):
    rows = SPLIT * TILE
    far[...] = keep[rows:] + arrived[rows:]
    near[...] = keep[:rows] + arrived[:rows]


def relay_kernel(arrived, out):
    out[...] = arrived[...]


def wholes_kernel(keep, arrived, *outs):
    for out, (first, tiles) in zip(outs, PARTS):
        rows = pl.ds(first * TILE, tiles * TILE)
        out[...] = keep[rows, :] + arrived[rows, :]


def apply_items(tiles, one, two, held, out, at, state_row, first=0):
    for tile in range(tiles):
        rows = pl.ds(tile * TILE, TILE)
        behind = held.shape[0] - 8 + first + tile
        new, column = descend(
            held[(first + tile) * TILE : (first + tile + 1) * TILE, :],
            column_of(held[behind : behind + 1, :TILE]),
            one[rows, :] + two[rows, :],
            item_rate,
        )
        out[at + tile * TILE : at + (tile + 1) * TILE, :] = new
        put_state(out, state_row + tile, column)


def step_kernel(tiles, first, one, two, held, *refs):
    out = refs[-1]
    rows = tiles * TILE
    out[rows : rows + 8, :] = jnp.zeros((8, WIDTH), F32)
    apply_items(tiles, one, two, held, out, 0, rows, first)


def join_kernel(one, two, held, done, out):
    rows = SPLIT * TILE
    out[:rows] = done[:rows]
    out[SHARE : SHARE + 8, :] = jnp.zeros((8, WIDTH), F32)
    out[SHARE : SHARE + SPLIT, :] = done[rows : rows + SPLIT, :]
    apply_items(HALF - SPLIT, one, two, held, out, rows, SHARE + SPLIT)


def place_kernel(part, *refs):
    core, _ = places()
    first, tiles = PARTS[part]
    own, other, *_, items_out, state_out, sems = refs
    rows = tiles * TILE
    copies = []
    for half, source in ((core, own), (1 - core, other)):
        start = pl.multiple_of(half * SHARE + first * TILE, TILE)
        for piece in range(2):
            copies.append(
                pltpu.make_async_copy(
                    source.at[pl.ds(piece * rows // 2, rows // 2), :],
                    items_out.at[pl.ds(start + piece * rows // 2, rows // 2), :],
                    sems.at[len(copies)],
                )
            )
            copies[-1].start()
    if part > 0:
        state_out[...] = refs[3][...]
    else:
        state_out[...] = jnp.zeros_like(state_out)
    for half, source in ((core, own), (1 - core, other)):
        for tile in range(tiles):
            place = half * HALF + first + tile
            state_out[place // 4, pl.ds(place % 4, 1), :] = source[
                rows + tile : rows + tile + 1, :TILE
            ]
    for copy in copies:
        copy.wait()


def struct(*shape, dtype=F32):
    return jax.ShapeDtypeStruct(shape, dtype)


ANY = pl.BlockSpec(memory_space=pl.ANY)
HBM = pl.BlockSpec(memory_space=pltpu.HBM)
VMEM = pl.BlockSpec(memory_space=pltpu.VMEM)


def call(body, name, in_specs, outs, *args, out_specs=None, scratch=(), limit=8,
         work=2_000_000, aliases=None):
    return pl.pallas_call(
        body,
        out_shape=outs,
        in_specs=in_specs,
        out_specs=jax.tree.map(lambda _: VMEM, outs) if out_specs is None else out_specs,
        scratch_shapes=scratch,
        input_output_aliases=aliases or {},
        compiler_params=pltpu.CompilerParams(vmem_limit_bytes=limit * 1024 * 1024),
        cost_estimate=pl.CostEstimate(flops=work, bytes_accessed=1_000_000, transcendentals=0),
        name=name,
    )(*args)


def run_grads(sweep, lists, count, ratings, users, *parts):
    share = struct(SHARE, WIDTH)
    scratch = [
        pltpu.SMEM(lists.shape[1:], jnp.int32),
        pltpu.SMEM(count.shape, jnp.int32),
        pltpu.VMEM((ROWS, WIDTH), BF16),
        pltpu.VMEM((SLOTS, ROWS, TILE), F32),
        pltpu.VMEM(ratings.shape[1:], BF16),
        pltpu.VMEM(users.shape, F32),
        pltpu.SemaphoreType.DMA((5,)),
    ]
    outs = [share, share]
    specs = [VMEM, VMEM]
    users_spec = ANY
    if sweep == 0:
        scratch += [
            pltpu.VMEM((SLOTS, TILE, WIDTH), F32),
            pltpu.VMEM((SHARE, WIDTH), F32),
            pltpu.VMEM((SHARE, WIDTH), F32),
            pltpu.VMEM((SLOTS, ROWS, TILE), F32),
            pltpu.VMEM((SLOTS, TILE, WIDTH), BF16),
            pltpu.SemaphoreType.DMA((HALF + 2,)),
        ]
        specs = [HBM]
        users_spec = HBM
    return call(
        functools.partial(grads_kernel, sweep),
        "grads",
        [HBM, HBM, HBM, users_spec] + specs,
        outs + [struct(SLOTS, ROWS, TILE), struct(SLOTS, TILE, WIDTH, dtype=BF16)],
        lists,
        count,
        ratings,
        users,
        *parts,
        out_specs=[HBM if sweep == 0 else VMEM] * 4,
        scratch=scratch,
        limit=LIMITS[sweep],
        work=2_000_000_000,
    )


def run_users(after, errors, items_low, users, state):
    return call(
        users_kernel,
        "users",
        [ANY] + [VMEM] * 4,
        [struct(*users.shape), struct(*state.shape), struct(8, TILE)],
        after,
        errors,
        items_low,
        users,
        state,
        limit=16,
        work=1_000_000_000,
    )


def per_device(
    user_factors, user_state, item_factors, item_state, tile_lists, tile_counts, ratings
):
    strata = lax.axis_size("blk")
    pairs = [(b, r) for b in range(strata) for r in range(4)]
    to_core = [(4 * b + r, 4 * b + (r ^ 1)) for b, r in pairs]
    to_chip = [(4 * b + r, 4 * b + (r ^ 2)) for b, r in pairs]
    turn = strata // 2

    def landing(b, r):
        if (b + 1) % turn == 0:
            swap = r % 2 if b + 1 == turn else 1 - r % 2
            return r ^ (2 * swap)
        return r

    to_next = [(4 * b + r, 4 * ((b + 1) % strata) + landing(b, r)) for b, r in pairs]

    def move(array, way):
        return lax.ppermute(array, ("blk", "rep"), way)

    items = item_factors.reshape(SLOTS, TILE, WIDTH)
    lists = tile_lists.transpose(0, 2, 1)
    count = tile_counts.T
    near_rows, far_rows = SPLIT * TILE, (HALF - SPLIT) * TILE

    send, keep, errors, low = run_grads(0, lists, count, ratings, user_factors, items)
    arrived = move(send, to_core)
    keep, hold, early = call(
        olds_kernel,
        "olds",
        [VMEM] * 3,
        [struct(SHARE, WIDTH), struct(near_rows + 8, WIDTH), struct(far_rows + 8, WIDTH)],
        keep,
        items,
        item_state,
    )
    old = move(early, to_next)
    near, far = call(
        parts_kernel,
        "parts",
        [VMEM] * 2,
        [struct(near_rows, WIDTH), struct(far_rows, WIDTH)],
        keep,
        arrived,
    )
    near_back = move(near, to_chip)
    far = move(far, to_next)
    far = call(relay_kernel, "relay", [VMEM], struct(far_rows, WIDTH), far, work=RELAY_WORK)
    users, ustate, _ = run_users(near, errors, low, user_factors, user_state)
    load = call(
        functools.partial(step_kernel, SPLIT, 0),
        "near_step",
        [VMEM] * 3,
        struct(near_rows + 8, WIDTH),
        near,
        near_back,
        hold,
    )
    done = move(load, to_next)
    far_back = move(far, to_chip)
    own = call(
        join_kernel, "join", [VMEM] * 4, struct(SHARE + 8, WIDTH), far, far_back, old, done
    )
    other = move(own, to_core)

    send, keep, errors, low = run_grads(1, lists, count, ratings, users, own, other)
    arrived = move(send, to_core)
    totals = call(
        wholes_kernel,
        "wholes",
        [VMEM] * 2,
        [struct(tiles * TILE, WIDTH) for _, tiles in PARTS],
        keep,
        arrived,
    )
    backs = [move(total, to_chip) for total in totals]
    users, ustate, token = run_users(totals[0], errors, low, users, ustate)
    news, others = [], []
    for (first, tiles), total, back in zip(PARTS, totals, backs):
        news.append(
            call(
                functools.partial(step_kernel, tiles, first),
                "last_step",
                [VMEM] * 3 + [ANY],
                struct(tiles * TILE + 8, WIDTH),
                total,
                back,
                own,
                token,
            )
        )
        others.append(move(news[-1], to_core))
    placed = ()
    for part in range(len(PARTS)):
        placed = call(
            functools.partial(place_kernel, part),
            "place",
            [VMEM, VMEM] + [HBM, VMEM] * (part > 0),
            [struct(2 * SHARE, WIDTH), struct(*item_state.shape)],
            news[part],
            others[part],
            *placed,
            out_specs=[HBM, VMEM],
            scratch=[pltpu.SemaphoreType.DMA((4,))],
            aliases={2: 0} if part > 0 else {},
        )
    items_out, state_out = placed
    return (users, ustate, items_out.reshape(item_factors.shape), state_out)


def solution(mesh):
    placed = (
        P("blk", "rep", None),
        P("blk", "rep"),
        P(None, "blk", None, None),
        P(None, "blk", None),
        P(None, "blk", None),
        P(None, "blk"),
        P(None, "blk", "rep", None),
    )
    return jax.shard_map(
        per_device,
        mesh=mesh,
        in_specs=placed,
        out_specs=(
            P("blk", "rep", None),
            P("blk", "rep"),
            P(None, "blk", None, None),
            P(None, "blk", None),
        ),
        check_vma=False,
    )
```

time: 448 us -> 97.4 us (0.22)
  waiting for transfers between devices: 169 us -> 37.9 us
  other arithmetic: 125 us -> 0 us
  local copies, waits for them, and re-layouts: 78.6 us -> 1.17 us
  matrix products: 51.6 us -> 0 us
  starting transfers between devices: 5.16 us -> 41.1 us
  Pallas kernels: 0 us -> 16.4 us
  between operations: 14.2 us -> 0.91 us
    psum x2 -> x0, waiting for transfers between devices: 131 us -> none  [per_device(): summed = lax.psum(grad_items, 'rep')]
    scatter-add x32 -> x0, other arithmetic: 90.8 us -> none  [the longest x16 69.4 us: step(): grad_items = grad_items.at[slot].add(item_terms)]
    dot_general x48 -> x0, matrix products: 51.6 us -> none  [the longest x16 23.3 us: step(): jnp.einsum('nrc,nrk->nck', error, user_tiles, preferred_element_type=jnp....]
    ppermute x2 -> x12, starting transfers between devices: 5.08 us -> 41.1 us  [move(): return lax.ppermute(array, ('blk', 'rep'), way)]
    gather x32 -> x0, local copies, waits for them, and re-layouts: 34 us -> none  [the longest x16 24.2 us: step(): user_tiles = jnp.take(users_low, user_index, axis=0)]
    dynamic_slice x32 -> x0, local copies, waits for them, and re-layouts: 21 us -> none  [tile_grads(): (grad_users, grad_items), unused = lax.scan(step, start, packs)]
    select_n x48 -> x0, other arithmetic: 19.1 us -> none  [the longest x16 18.9 us: step(): jnp.where(live, entries[:, 3].astype(jnp.float32) * 0.25, jnp.float32(0.0))]
    pallas_call x0 -> x14, Pallas kernels: none -> 16.4 us  [call(): pl.pallas_call(body, out_shape=outs, in_specs=in_specs, out_specs=jax.tre...]
  transfers between devices with their start and end apart: 4 -> 12, of which waited for: 3 -> 10; matrix products, arithmetic and copies ran while one was open for 1% -> 0% of each run, Pallas kernels for 0% -> 8%
where the time goes in v2:
time: 97.4 us
  starting transfers between devices  41.1 us (42%)
  waiting for transfers between devices  37.9 us (39%)
  Pallas kernels  16.4 us (17%)
  local copies, waits for them, and re-layouts  1.17 us (1%)
    ppermute x12, starting transfers between devices, move(): return lax.ppermute(array, ('blk', 'rep'), way)  41.1 us
    ppermute x12, waiting for transfers between devices, move(): return lax.ppermute(array, ('blk', 'rep'), way)  37.9 us
    pallas_call x14, Pallas kernels, call(): pl.pallas_call(body, out_shape=outs, in_specs=in_specs, out_specs=jax.tre...  16.4 us
  transfers between devices with their start and end apart: 12, of which 10 were waited for; matrix products, arithmetic and copies ran while one was open for 0% of the time, Pallas kernels for 8%

profile of v2, /device:TPU:1, one launch (start us, length us, event | category | flops | bytes accessed | tf_op | source)
XLA Modules:
  0.0 97.4 jit_solution(14777184592468215410)
XLA Ops:
  0.7 4.7 %grads.2 = (f32[768,256]{1,0:T(8,128)}, f32[768,256]{1,0:T(8,128)}, f32[12,512,128]{2,1,0:T(8,128)}, bf16[12,128,256]{2,1,0:T(8,128)(2,1)}) custom-call(s32[2,4,128]{2,1,0:T(4,128)} %bitcast.6, s32[1,2]{1,0:T(1,128)} %bitcast.8, bf16[2,128,32,128]{3,2,1,0:T(8,128)(2,1)} %ratings.3, f32[16,32,256]{2,1,0:T(8,128)} %users.6, f32[12,128,256]{2,1,0:T(8,128)} %bitcast.4), custom_call_target="tpu_custom_call" | custom-call | flops 2000000000 | bytes 1000000 | tf_op jit(solution)/shard_map/grads/pallas_call | solution.py:269
  5.3 8.8 %collective-permute-start = (f32[768,256]{1,0:T(8,128)}, f32[768,256]{1,0:T(8,128)S(1)}, u32[]{:S(2)}, u32[]{:S(2)}) collective-permute-start(f32[768,256]{1,0:T(8,128)} %get-tuple-element.30), channel_id=1, source_target_pairs={{0,1},{1,0},{2,3},{3,2},{4,5},{5,4},{6,7},{7,6},{8,9},{9,8},{10,11... | collective-permute-start | bytes 2359304 | tf_op jit(solution)/shard_map/ppermute | solution.py:358
  14.2 1.1 %copy-done.3 = f32[768,256]{1,0:T(8,128)S(1)} copy-done((f32[768,256]{1,0:T(8,128)S(1)}, f32[768,256]{1,0:T(8,128)}, u32[]{:S(2)}) %copy-start.3) | copy-done | bytes 786456
  15.4 0.8 collective-permute-done.arrived
  16.3 1.9 %collective-permute-start.4 = (f32[512,256]{1,0:T(8,128)S(1)}, f32[512,256]{1,0:T(8,128)S(1)}, u32[]{:S(2)}, u32[]{:S(2)}) collective-permute-start(f32[512,256]{1,0:T(8,128)S(1)} %get-tuple-element.31.after.one), channel_id=1, source_target_pairs={{0,2},{1,3},{2,0},{3,1},{4,6},{5,7},{6,4},{7,5},{8,10},{9,11},{10,... | collective-permute-start | bytes 1572872 | tf_op jit(solution)/shard_map/ppermute | solution.py:358
  18.3 1.9 %collective-permute-start.1 = (f32[256,256]{1,0:T(8,128)S(1)}, f32[256,256]{1,0:T(8,128)S(1)}, u32[]{:S(2)}, u32[]{:S(2)}) collective-permute-start(f32[256,256]{1,0:T(8,128)S(1)} %get-tuple-element.35), channel_id=1, source_target_pairs={{0,4},{1,5},{2,6},{3,7},{4,8},{5,9},{6,10},{7,11},{8,12},{9,13},{1... | collective-permute-start | bytes 786440 | tf_op jit(solution)/shard_map/ppermute | solution.py:358
  20.2 2.6 %collective-permute-start.3 = (f32[264,256]{1,0:T(8,128)S(1)}, f32[264,256]{1,0:T(8,128)S(1)}, u32[]{:S(2)}, u32[]{:S(2)}) collective-permute-start(f32[264,256]{1,0:T(8,128)S(1)} %get-tuple-element.36), channel_id=1, source_target_pairs={{0,4},{1,5},{2,6},{3,7},{4,8},{5,9},{6,10},{7,11},{8,12},{9,13},{1... | collective-permute-start | bytes 811016 | tf_op jit(solution)/shard_map/ppermute | solution.py:358
  22.8 10.1 %collective-permute-done.4.two = f32[512,256]{1,0:T(8,128)S(1)} collective-permute-done((f32[512,256]{1,0:T(8,128)S(1)}, f32[512,256]{1,0:T(8,128)S(1)}, u32[]{:S(2)}, u32[]{:S(2)}) %collective-permute-start.4) | collective-permute-done | bytes 524320 | tf_op jit(solution)/shard_map/ppermute | solution.py:358
  32.9 0.6 near_step.1
  33.4 1.9 %collective-permute-start.5 = (f32[520,256]{1,0:T(8,128)S(1)}, f32[520,256]{1,0:T(8,128)S(1)}, u32[]{:S(2)}, u32[]{:S(2)}) collective-permute-start(f32[520,256]{1,0:T(8,128)S(1)} %near_step.1), channel_id=1, source_target_pairs={{0,4},{1,5},{2,6},{3,7},{4,8},{5,9},{6,10},{7,11},{8,12},{9,13},{1... | collective-permute-start | bytes 1597448 | tf_op jit(solution)/shard_map/ppermute | solution.py:358
  35.4 0.9 collective-permute-done.1.arrived
  36.4 3.9 %collective-permute-start.2 = (f32[256,256]{1,0:T(8,128)S(1)}, f32[256,256]{1,0:T(8,128)S(1)}, u32[]{:S(2)}, u32[]{:S(2)}) collective-permute-start(f32[256,256]{1,0:T(8,128)S(1)} %relay.1.one), channel_id=1, source_target_pairs={{0,2},{1,3},{2,0},{3,1},{4,6},{5,7},{6,4},{7,5},{8,10},{9,11},{10,... | collective-permute-start | bytes 786440 | tf_op jit(solution)/shard_map/ppermute | solution.py:358
  40.3 1.8 %collective-permute-done.3.held = f32[264,256]{1,0:T(8,128)S(1)} collective-permute-done((f32[264,256]{1,0:T(8,128)S(1)}, f32[264,256]{1,0:T(8,128)S(1)}, u32[]{:S(2)}, u32[]{:S(2)}) %collective-permute-start.3) | collective-permute-done | bytes 270368 | tf_op jit(solution)/shard_map/ppermute | solution.py:358
  42.1 3.1 %collective-permute-done.2.two = f32[256,256]{1,0:T(8,128)S(1)} collective-permute-done((f32[256,256]{1,0:T(8,128)S(1)}, f32[256,256]{1,0:T(8,128)S(1)}, u32[]{:S(2)}, u32[]{:S(2)}) %collective-permute-start.2) | collective-permute-done | bytes 262176 | tf_op jit(solution)/shard_map/ppermute | solution.py:358
  45.3 9.6 %collective-permute-done.5.done = f32[520,256]{1,0:T(8,128)S(1)} collective-permute-done((f32[520,256]{1,0:T(8,128)S(1)}, f32[520,256]{1,0:T(8,128)S(1)}, u32[]{:S(2)}, u32[]{:S(2)}) %collective-permute-start.5) | collective-permute-done | bytes 532512 | tf_op jit(solution)/shard_map/ppermute | solution.py:358
  54.8 0.4 join.1.refs_0_.held
  55.2 5.0 %collective-permute-start.6 = (f32[776,256]{1,0:T(8,128)S(1)}, f32[776,256]{1,0:T(8,128)S(1)}, u32[]{:S(2)}, u32[]{:S(2)}) collective-permute-start(f32[776,256]{1,0:T(8,128)S(1)} %join.1.refs_0_.held), channel_id=1, source_target_pairs={{0,1},{1,0},{2,3},{3,2},{4,5},{5,4},{6,7},{7,6},{8,9},{9,8},{10,11... | collective-permute-start | bytes 2383880 | tf_op jit(solution)/shard_map/ppermute | solution.py:358
  60.3 2.2 %users.5 = (f32[16,32,256]{2,1,0:T(8,128)S(1)}, f32[16,32]{1,0:T(8,128)S(1)}, f32[8,128]{1,0:T(8,128)}) custom-call(f32[512,256]{1,0:T(8,128)S(1)} %get-tuple-element.31.after.one, f32[12,512,128]{2,1,0:T(8,128)S(1)} %copy-done, bf16[12,128,256]{2,1,0:T(8,128)(2,1)S(1)} %copy-done.2, f32[16,32,256]{2,1,0:T(8,128)S(1)} %copy-done.4, f32[16,32]{1,0:T(8,128)S(1)} %copy-done.5), custom_call_target="tpu_custom_call" | custom-call | flops 1000000000 | bytes 1000000 | tf_op jit(solution)/shard_map/users/pallas_call | solution.py:269
  62.6 2.4 %grads.3 = (f32[768,256]{1,0:T(8,128)S(1)}, f32[768,256]{1,0:T(8,128)S(1)}, f32[12,512,128]{2,1,0:T(8,128)S(1)}, bf16[12,128,256]{2,1,0:T(8,128)(2,1)S(1)}) custom-call(s32[2,4,128]{2,1,0:T(4,128)S(1)} %bitcast.7, s32[1,2]{1,0:T(1,128)S(1)} %bitcast.9, bf16[2,128,32,128]{3,2,1,0:T(8,128)(2,1)S(1)} %copy-done.7, f32[16,32,256]{2,1,0:T(8,128)S(1)} %get-tuple-element.34.users, ...), custom_call_target="tpu_custom_call" | custom-call | flops 2000000000 | bytes 1000000 | tf_op jit(solution)/shard_map/grads/pallas_call | solution.py:269
  64.9 1.9 %collective-permute-start.7 = (f32[768,256]{1,0:T(8,128)S(1)}, f32[768,256]{1,0:T(8,128)S(1)}, u32[]{:S(2)}, u32[]{:S(2)}) collective-permute-start(f32[768,256]{1,0:T(8,128)S(1)} %get-tuple-element.39), channel_id=1, source_target_pairs={{0,1},{1,0},{2,3},{3,2},{4,5},{5,4},{6,7},{7,6},{8,9},{9,8},{10,11... | collective-permute-start | bytes 2359304 | tf_op jit(solution)/shard_map/ppermute | solution.py:358
  66.8 2.3 %collective-permute-done.7.arrived = f32[768,256]{1,0:T(8,128)S(1)} collective-permute-done((f32[768,256]{1,0:T(8,128)S(1)}, f32[768,256]{1,0:T(8,128)S(1)}, u32[]{:S(2)}, u32[]{:S(2)}) %collective-permute-start.7) | collective-permute-done | bytes 786464 | tf_op jit(solution)/shard_map/ppermute | solution.py:358
  69.2 3.2 %collective-permute-start.10 = (f32[512,256]{1,0:T(8,128)S(1)}, f32[512,256]{1,0:T(8,128)S(1)}, u32[]{:S(2)}, u32[]{:S(2)}) collective-permute-start(f32[512,256]{1,0:T(8,128)S(1)} %get-tuple-element.40.after.one), channel_id=1, source_target_pairs={{0,2},{1,3},{2,0},{3,1},{4,6},{5,7},{6,4},{7,5},{8,10},{9,11},{10,... | collective-permute-start | bytes 1572872 | tf_op jit(solution)/shard_map/ppermute | solution.py:358
  72.4 3.6 %collective-permute-start.8 = (f32[256,256]{1,0:T(8,128)S(1)}, f32[256,256]{1,0:T(8,128)S(1)}, u32[]{:S(2)}, u32[]{:S(2)}) collective-permute-start(f32[256,256]{1,0:T(8,128)S(1)} %get-tuple-element.46.one), channel_id=1, source_target_pairs={{0,2},{1,3},{2,0},{3,1},{4,6},{5,7},{6,4},{7,5},{8,10},{9,11},{10,... | collective-permute-start | bytes 786440 | tf_op jit(solution)/shard_map/ppermute | solution.py:358
  76.0 2.5 %users.7 = (f32[16,32,256]{2,1,0:T(8,128)}, f32[16,32]{1,0:T(8,128)}, f32[8,128]{1,0:T(8,128)S(1)}) custom-call(f32[512,256]{1,0:T(8,128)S(1)} %get-tuple-element.40.after.one, f32[12,512,128]{2,1,0:T(8,128)S(1)} %get-tuple-element.41.errors, bf16[12,128,256]{2,1,0:T(8,128)(2,1)S(1)} %get-tuple-element.42.items_low, ...), custom_call_target="tpu_custom_call" | custom-call | flops 1000000000 | bytes 1000000 | tf_op jit(solution)/shard_map/users/pallas_call | solution.py:269
  78.5 7.5 %collective-permute-done.10.two = f32[512,256]{1,0:T(8,128)S(1)} collective-permute-done((f32[512,256]{1,0:T(8,128)S(1)}, f32[512,256]{1,0:T(8,128)S(1)}, u32[]{:S(2)}, u32[]{:S(2)}) %collective-permute-start.10) | collective-permute-done | bytes 524320 | tf_op jit(solution)/shard_map/ppermute | solution.py:358
  86.0 0.6 last_step.3.refs_0_
  86.5 3.4 %collective-permute-start.11 = (f32[520,256]{1,0:T(8,128)S(1)}, f32[520,256]{1,0:T(8,128)S(1)}, u32[]{:S(2)}, u32[]{:S(2)}) collective-permute-start(f32[520,256]{1,0:T(8,128)S(1)} %last_step.3.refs_0_), channel_id=1, source_target_pairs={{0,1},{1,0},{2,3},{3,2},{4,5},{5,4},{6,7},{7,6},{8,9},{9,8},{10,11... | collective-permute-start | bytes 1597448 | tf_op jit(solution)/shard_map/ppermute | solution.py:358
  90.0 1.6 %collective-permute-done.8.two = f32[256,256]{1,0:T(8,128)S(1)} collective-permute-done((f32[256,256]{1,0:T(8,128)S(1)}, f32[256,256]{1,0:T(8,128)S(1)}, u32[]{:S(2)}, u32[]{:S(2)}) %collective-permute-start.8) | collective-permute-done | bytes 262176 | tf_op jit(solution)/shard_map/ppermute | solution.py:358
  91.6 0.4 last_step.2.refs_0_
  92.0 2.9 %collective-permute-start.9 = (f32[264,256]{1,0:T(8,128)S(1)}, f32[264,256]{1,0:T(8,128)S(1)}, u32[]{:S(2)}, u32[]{:S(2)}) collective-permute-start(f32[264,256]{1,0:T(8,128)S(1)} %last_step.2.refs_0_), channel_id=1, source_target_pairs={{0,1},{1,0},{2,3},{3,2},{4,5},{5,4},{6,7},{7,6},{8,9},{9,8},{10,11... | collective-permute-start | bytes 811016 | tf_op jit(solution)/shard_map/ppermute | solution.py:358
  94.8 1.0 %place.2 = (f32[1536,256]{1,0:T(8,128)}, f32[3,4,128]{2,1,0:T(4,128)S(1)}) custom-call(f32[520,256]{1,0:T(8,128)S(1)} %last_step.3.refs_0_, f32[520,256]{1,0:T(8,128)S(1)} %collective-permute-done.11.refs_1_), custom_call_target="tpu_custom_call" | custom-call | flops 2000000 | bytes 1000000 | tf_op jit(solution)/shard_map/place/pallas_call | solution.py:269
  96.0 1.4 %place.3 = (f32[1536,256]{1,0:T(8,128)}, f32[3,4,128]{2,1,0:T(4,128)}) custom-call(f32[264,256]{1,0:T(8,128)S(1)} %last_step.2.refs_0_, f32[264,256]{1,0:T(8,128)S(1)} %collective-permute-done.9.refs_1_, f32[1536,256]{1,0:T(8,128)} %get-tuple-element.48.refs_2_, f32[3,4,128]{2,1,0:T(4,128)S(1)} %get-tuple-element.49.refs_3_), custom_call_target="tpu_custom_call", output_to_operand_aliasing={{0}: (2, {})} | custom-call | flops 2000000 | bytes 1000000 | tf_op jit(solution)/shard_map/place/pallas_call | solution.py:269
  (26 shorter events, 0.5 us)
Async XLA Ops:
  0.6 13.5 %copy-start.1 = (f32[3,4,128,256]{3,2,1,0:T(8,128)S(1)}, f32[3,4,128,256]{3,2,1,0:T(8,128)}, u32[]{:S(2)}) copy-start(f32[3,4,128,256]{3,2,1,0:T(8,128)} %param.9) | copy-start | bytes 4718596
  0.6 13.5 %copy-start.6 = (f32[3,4,128]{2,1,0:T(4,128)S(1)}, f32[3,4,128]{2,1,0:T(4,128)}, u32[]{:S(2)}) copy-start(f32[3,4,128]{2,1,0:T(4,128)} %states.1) | copy-start | bytes 18436
  5.3 10.9 %collective-permute-start = (f32[768,256]{1,0:T(8,128)}, f32[768,256]{1,0:T(8,128)S(1)}, u32[]{:S(2)}, u32[]{:S(2)}) collective-permute-start(f32[768,256]{1,0:T(8,128)} %get-tuple-element.30), channel_id=1, source_target_pairs={{0,1},{1,0},{2,3},{3,2},{4,5},{5,4},{6,7},{7,6},{8,9},{9,8},{10,11... | collective-permute-start | bytes 2359304 | tf_op jit(solution)/shard_map/ppermute | solution.py:358
  14.2 1.1 %copy-start.3 = (f32[768,256]{1,0:T(8,128)S(1)}, f32[768,256]{1,0:T(8,128)}, u32[]{:S(2)}) copy-start(f32[768,256]{1,0:T(8,128)} %get-tuple-element.28.keep) | copy-start | bytes 2359300
  16.3 16.5 %collective-permute-start.4 = (f32[512,256]{1,0:T(8,128)S(1)}, f32[512,256]{1,0:T(8,128)S(1)}, u32[]{:S(2)}, u32[]{:S(2)}) collective-permute-start(f32[512,256]{1,0:T(8,128)S(1)} %get-tuple-element.31.after.one), channel_id=1, source_target_pairs={{0,2},{1,3},{2,0},{3,1},{4,6},{5,7},{6,4},{7,5},{8,10},{9,11},{10,... | collective-permute-start | bytes 1572872 | tf_op jit(solution)/shard_map/ppermute | solution.py:358
  18.3 18.1 %collective-permute-start.1 = (f32[256,256]{1,0:T(8,128)S(1)}, f32[256,256]{1,0:T(8,128)S(1)}, u32[]{:S(2)}, u32[]{:S(2)}) collective-permute-start(f32[256,256]{1,0:T(8,128)S(1)} %get-tuple-element.35), channel_id=1, source_target_pairs={{0,4},{1,5},{2,6},{3,7},{4,8},{5,9},{6,10},{7,11},{8,12},{9,13},{1... | collective-permute-start | bytes 786440 | tf_op jit(solution)/shard_map/ppermute | solution.py:358
  20.2 21.9 %collective-permute-start.3 = (f32[264,256]{1,0:T(8,128)S(1)}, f32[264,256]{1,0:T(8,128)S(1)}, u32[]{:S(2)}, u32[]{:S(2)}) collective-permute-start(f32[264,256]{1,0:T(8,128)S(1)} %get-tuple-element.36), channel_id=1, source_target_pairs={{0,4},{1,5},{2,6},{3,7},{4,8},{5,9},{6,10},{7,11},{8,12},{9,13},{1... | collective-permute-start | bytes 811016 | tf_op jit(solution)/shard_map/ppermute | solution.py:358
  33.4 21.4 %collective-permute-start.5 = (f32[520,256]{1,0:T(8,128)S(1)}, f32[520,256]{1,0:T(8,128)S(1)}, u32[]{:S(2)}, u32[]{:S(2)}) collective-permute-start(f32[520,256]{1,0:T(8,128)S(1)} %near_step.1), channel_id=1, source_target_pairs={{0,4},{1,5},{2,6},{3,7},{4,8},{5,9},{6,10},{7,11},{8,12},{9,13},{1... | collective-permute-start | bytes 1597448 | tf_op jit(solution)/shard_map/ppermute | solution.py:358
  36.3 23.9 %copy-start = (f32[12,512,128]{2,1,0:T(8,128)S(1)}, f32[12,512,128]{2,1,0:T(8,128)}, u32[]{:S(2)}) copy-start(f32[12,512,128]{2,1,0:T(8,128)} %get-tuple-element.32.errors) | copy-start | bytes 9437188
  36.3 23.9 %copy-start.2 = (bf16[12,128,256]{2,1,0:T(8,128)(2,1)S(1)}, bf16[12,128,256]{2,1,0:T(8,128)(2,1)}, u32[]{:S(2)}) copy-start(bf16[12,128,256]{2,1,0:T(8,128)(2,1)} %get-tuple-element.33.items_low) | copy-start | bytes 2359300
  36.3 23.9 %copy-start.4 = (f32[16,32,256]{2,1,0:T(8,128)S(1)}, f32[16,32,256]{2,1,0:T(8,128)}, u32[]{:S(2)}) copy-start(f32[16,32,256]{2,1,0:T(8,128)} %users.6) | copy-start | bytes 1572868
  36.4 23.9 %copy-start.5 = (f32[16,32]{1,0:T(8,128)S(1)}, f32[16,32]{1,0:T(8,128)}, u32[]{:S(2)}) copy-start(f32[16,32]{1,0:T(8,128)} %state.1) | copy-start | bytes 6148
  36.4 8.9 %collective-permute-start.2 = (f32[256,256]{1,0:T(8,128)S(1)}, f32[256,256]{1,0:T(8,128)S(1)}, u32[]{:S(2)}, u32[]{:S(2)}) collective-permute-start(f32[256,256]{1,0:T(8,128)S(1)} %relay.1.one), channel_id=1, source_target_pairs={{0,2},{1,3},{2,0},{3,1},{4,6},{5,7},{6,4},{7,5},{8,10},{9,11},{10,... | collective-permute-start | bytes 786440 | tf_op jit(solution)/shard_map/ppermute | solution.py:358
  55.2 7.3 %collective-permute-start.6 = (f32[776,256]{1,0:T(8,128)S(1)}, f32[776,256]{1,0:T(8,128)S(1)}, u32[]{:S(2)}, u32[]{:S(2)}) collective-permute-start(f32[776,256]{1,0:T(8,128)S(1)} %join.1.refs_0_.held), channel_id=1, source_target_pairs={{0,1},{1,0},{2,3},{3,2},{4,5},{5,4},{6,7},{7,6},{8,9},{9,8},{10,11... | collective-permute-start | bytes 2383880 | tf_op jit(solution)/shard_map/ppermute | solution.py:358
  60.3 2.3 %copy-start.7 = (bf16[2,128,32,128]{3,2,1,0:T(8,128)(2,1)S(1)}, bf16[2,128,32,128]{3,2,1,0:T(8,128)(2,1)}, u32[]{:S(2)}) copy-start(bf16[2,128,32,128]{3,2,1,0:T(8,128)(2,1)} %ratings.3) | copy-start | bytes 6291460
  60.3 2.3 %copy-start.8 = (s32[2,128,4]{1,2,0:T(4,128)S(1)}, s32[2,128,4]{1,2,0:T(4,128)}, u32[]{:S(2)}) copy-start(s32[2,128,4]{1,2,0:T(4,128)} %param.11) | copy-start | bytes 12292
  60.3 2.3 %copy-start.9 = (s32[2,1]{0,1:T(1,128)S(1)}, s32[2,1]{0,1:T(1,128)}, u32[]{:S(2)}) copy-start(s32[2,1]{0,1:T(1,128)} %param.12) | copy-start | bytes 28
  64.9 4.2 %collective-permute-start.7 = (f32[768,256]{1,0:T(8,128)S(1)}, f32[768,256]{1,0:T(8,128)S(1)}, u32[]{:S(2)}, u32[]{:S(2)}) collective-permute-start(f32[768,256]{1,0:T(8,128)S(1)} %get-tuple-element.39), channel_id=1, source_target_pairs={{0,1},{1,0},{2,3},{3,2},{4,5},{5,4},{6,7},{7,6},{8,9},{9,8},{10,11... | collective-permute-start | bytes 2359304 | tf_op jit(solution)/shard_map/ppermute | solution.py:358
  69.2 16.8 %collective-permute-start.10 = (f32[512,256]{1,0:T(8,128)S(1)}, f32[512,256]{1,0:T(8,128)S(1)}, u32[]{:S(2)}, u32[]{:S(2)}) collective-permute-start(f32[512,256]{1,0:T(8,128)S(1)} %get-tuple-element.40.after.one), channel_id=1, source_target_pairs={{0,2},{1,3},{2,0},{3,1},{4,6},{5,7},{6,4},{7,5},{8,10},{9,11},{10,... | collective-permute-start | bytes 1572872 | tf_op jit(solution)/shard_map/ppermute | solution.py:358
  72.4 19.2 %collective-permute-start.8 = (f32[256,256]{1,0:T(8,128)S(1)}, f32[256,256]{1,0:T(8,128)S(1)}, u32[]{:S(2)}, u32[]{:S(2)}) collective-permute-start(f32[256,256]{1,0:T(8,128)S(1)} %get-tuple-element.46.one), channel_id=1, source_target_pairs={{0,2},{1,3},{2,0},{3,1},{4,6},{5,7},{6,4},{7,5},{8,10},{9,11},{10,... | collective-permute-start | bytes 786440 | tf_op jit(solution)/shard_map/ppermute | solution.py:358
  86.5 8.3 %collective-permute-start.11 = (f32[520,256]{1,0:T(8,128)S(1)}, f32[520,256]{1,0:T(8,128)S(1)}, u32[]{:S(2)}, u32[]{:S(2)}) collective-permute-start(f32[520,256]{1,0:T(8,128)S(1)} %last_step.3.refs_0_), channel_id=1, source_target_pairs={{0,1},{1,0},{2,3},{3,2},{4,5},{5,4},{6,7},{7,6},{8,9},{9,8},{10,11... | collective-permute-start | bytes 1597448 | tf_op jit(solution)/shard_map/ppermute | solution.py:358
  92.0 4.0 %collective-permute-start.9 = (f32[264,256]{1,0:T(8,128)S(1)}, f32[264,256]{1,0:T(8,128)S(1)}, u32[]{:S(2)}, u32[]{:S(2)}) collective-permute-start(f32[264,256]{1,0:T(8,128)S(1)} %last_step.2.refs_0_), channel_id=1, source_target_pairs={{0,1},{1,0},{2,3},{3,2},{4,5},{5,4},{6,7},{7,6},{8,9},{9,8},{10,11... | collective-permute-start | bytes 811016 | tf_op jit(solution)/shard_map/ppermute | solution.py:358
